TPU v7x, 128 devices: a whole 4x4x4 slice. The times are simulated.
128 devices in a mesh: row: 16 (over x_lo, y, core), col: 8 (over z, x_hi).
Axes of the slice: x: 4 (x_hi: 2, x_lo: 2; x = x_hi * 2 + x_lo), y: 4, z: 4, core: 2. Of those that a mesh axis runs over, the one named last changes fastest.
Arguments:
- pair_map: float32 [1024, 1024, 128], P('row', 'col'), may hold values from -6 to 6
- valid_length: int32 [1], replicated, may hold values from 512 to 1024
- norm_gain: float32 [2, 2, 128], replicated, may hold values from 0.1 to 1.9
- norm_bias: float32 [2, 2, 128], replicated, may hold values from -1.5 to 1.5
- proj_weight: bfloat16 [2, 128, 4, 128], replicated, may hold values from -0.5 to 0.5
- gate_weight: bfloat16 [2, 128, 128], replicated, may hold values from -0.5 to 0.5
- out_weight: bfloat16 [2, 128, 128], replicated, may hold values from -0.5 to 0.5
Outputs:
- pair_out: float32 [1024, 1024, 128], P('row', 'col')
Inputs may be any that keep to these rules, and one draw needn't show every extreme that they name: Tokens from valid_length on are padding.
All inputs are finite; a program needn't handle non-finite values.
Results may differ from a plain program's by a relative error of at most 0.0039.
Values may be sent and summed in bfloat16 or wider, within the bound.
No kernel may reach another device: no remote copies, remote signals or barrier semaphores. Data moves between devices by JAX's collectives and lax.ppermute only.
A program may use at most 64 MiB of HBM per device.

v0:
```python
import jax
import jax.numpy as jnp
from jax import lax
from jax.sharding import PartitionSpec as P

epsilon = 1e-05


def layer_norm(values, gain, offset, axis):
    centre = jnp.mean(values, axis=axis, keepdims=True)
    centred = values - centre
    variance = jnp.mean(centred * centred, axis=axis, keepdims=True)
    return centred * lax.rsqrt(variance + epsilon) * gain + offset


def to_channel_layout(factors):
    return lax.all_to_all(
        lax.all_to_all(factors, "row", split_axis=1, concat_axis=2, tiled=True),
        "col",
        split_axis=1,
        concat_axis=3,
        tiled=True,
    )


def to_tile_layout(product, tile_rows, tile_cols):
    n_row = lax.axis_size("row")
    n_col = lax.axis_size("col")
    per_dev = product.shape[0]
    moved = lax.all_to_all(
        lax.all_to_all(product, "row", split_axis=1, concat_axis=0, tiled=True),
        "col",
        split_axis=2,
        concat_axis=0,
        tiled=True,
    )
    moved = moved.reshape(n_col, n_row, per_dev, tile_rows, tile_cols).transpose(1, 0, 2, 3, 4)
    return moved.reshape(n_row * n_col * per_dev, tile_rows, tile_cols)


def per_device(pair_map, valid_length, norm_gain, norm_bias, proj_weight, gate_weight, out_weight):
    tile_rows, tile_cols, channels = pair_map.shape
    row_pos = lax.axis_index("row") * tile_rows + jnp.arange(tile_rows, dtype=jnp.int32)
    col_pos = lax.axis_index("col") * tile_cols + jnp.arange(tile_cols, dtype=jnp.int32)
    limit = valid_length[0]
    mask = (row_pos < limit).astype(jnp.float32)[:, None] * (col_pos < limit).astype(jnp.float32)[
        None, :
    ]
    state = pair_map
    for layer in range(2):
        normed = layer_norm(state, norm_gain[layer, 0], norm_bias[layer, 0], -1).astype(
            jnp.bfloat16
        )
        projected = jnp.einsum(
            "rsc,cgd->gdrs", normed, proj_weight[layer], preferred_element_type=jnp.float32
        )
        factors = (jax.nn.sigmoid(projected[1::2]) * projected[0::2] * mask).astype(jnp.bfloat16)
        projected = None
        gathered = to_channel_layout(factors)
        if layer == 0:
            product = jnp.einsum(
                "cik,cjk->cij", gathered[0], gathered[1], preferred_element_type=jnp.float32
            )
        else:
            product = jnp.einsum(
                "cki,ckj->cij", gathered[0], gathered[1], preferred_element_type=jnp.float32
            )
        product = product.astype(jnp.bfloat16)
        returned = to_tile_layout(product, tile_rows, tile_cols)
        hidden = layer_norm(
            returned.astype(jnp.float32),
            norm_gain[layer, 1][:, None, None],
            norm_bias[layer, 1][:, None, None],
            0,
        ).astype(jnp.bfloat16)
        update_term = jnp.einsum(
            "crs,cd->rsd", hidden, out_weight[layer], preferred_element_type=jnp.float32
        )
        gate_value = jax.nn.sigmoid(
            jnp.einsum(
                "rsc,cd->rsd", normed, gate_weight[layer], preferred_element_type=jnp.float32
            )
        )
        state = state + gate_value * update_term
    return state


def solution(mesh):
    placed = (P("row", "col", None), P(), P(), P(), P(), P(), P())
    return jax.shard_map(
        per_device, mesh=mesh, in_specs=placed, out_specs=P("row", "col", None), check_vma=False
    )
```

profile of v0, /device:TPU:0, one launch (start us, length us, event | category | flops | bytes accessed | tf_op | source)
XLA Modules:
  0.0 542.8 jit_solution(17216300042493940940)
XLA Ops:
  0.0 3.4 reduce_sum.72
  3.4 3.9 multiply_reduce_fusion.3
  8.3 4.9 convolution_bitcast_fusion.1
  13.2 3.8 multiply_convert_fusion.1
  16.9 11.2 %copy.269 = bf16[2,128,64,128]{3,0,2,1:T(2,128)(2,1)} copy(bf16[2,128,64,128]{1,3,0,2:T(8,128)(2,1)} %multiply_convert_fusion.1) | data formatting | bytes 8388608 | tf_op jit(solution)/shard_map/convert_element_type | solution.py:57
  28.2 55.8 %all_to_all.108 = bf16[2,128,64,128]{3,0,2,1:T(2,128)(2,1)S(1)} all-to-all(bf16[2,128,64,128]{3,0,2,1:T(2,128)(2,1)} %copy.269), channel_id=1, replica_groups=mesh['row'=16,'col'=8] {'row'}, dimensions={1} | all-to-all | bytes 8388608 | tf_op jit(solution)/shard_map/all_to_all | solution.py:18
  83.9 1.1 copy.270
  85.1 1.4 copy.271
  86.8 57.9 %all_to_all.109 = bf16[2,8,1024,128]{3,2,0,1:T(8,128)(2,1)S(1)} all-to-all(bf16[2,8,1024,128]{3,2,0,1:T(8,128)(2,1)S(1)} %copy.272), channel_id=1, replica_groups=mesh['row'=16,'col'=8] {'col'}, dimensions={1} | all-to-all | bytes 8388608 | tf_op jit(solution)/shard_map/all_to_all | solution.py:17
  145.1 2.4 fusion.6
  147.5 5.2 copy.333
  152.7 0.5 broadcast.158
  153.2 12.7 %reduce.20 = bf16[1024,1024]{1,0:T(8,128)(2,1)S(1)} reduce(bf16[1024,1,1024]{2,1,0:T(2,128)(2,1)} %bitcast.167, bf16[]{:T(256)} %broadcast.158), dimensions={1}, to_apply=%bitcast.152.reduce_sub_computation | reduce | bytes 4194306
  165.9 2.8 reshape.190
  168.7 31.4 %all_to_all.110 = bf16[16,2,32768]{2,1,0:T(2,128)(2,1)S(1)} all-to-all(bf16[16,2,32768]{2,1,0:T(2,128)(2,1)} %reshape.190), channel_id=1, replica_groups=mesh['row'=16,'col'=8] {'row'}, dimensions={0} | all-to-all | bytes 4194304 | tf_op jit(solution)/shard_map/all_to_all | solution.py:31
  200.1 6.7 %reshape.191 = bf16[1024,1,1024]{2,1,0:T(2,128)(2,1)} reshape(bf16[16,2,32768]{2,1,0:T(2,128)(2,1)S(1)} %all_to_all.110) | data formatting | bytes 4194304
  206.8 3.0 copy.308
  209.8 4.8 copy.275
  214.6 7.6 %reshape.192 = bf16[8,2,65536]{2,1,0:T(2,128)(2,1)} reshape(bf16[1024,16,64]{2,1,0:T(8,128)(2,1)} %bitcast.170) | data formatting | bytes 4194304
  222.2 4.0 all-to-all-start.3
  226.2 5.6 %copy.284 = f32[64,128,128]{1,2,0:T(8,128)} copy(f32[64,128,128]{2,1,0:T(8,128)} %param.7) | data formatting | bytes 8388608 | tf_op args[0]
  232.0 6.3 %fusion.8 = f32[64,128,128]{1,2,0:T(8,128)} fusion(bf16[2,128,128]{2,1,0:T(8,128)(2,1)S(1)} %copy-done.6, f32[64,128,128]{2,1,0:T(8,128)} %param.7, f32[128]{0:T(128)S(1)} %get-tuple-element.18, f32[128]{0:T(128)S(1)} %get-tuple-element.25, f32[64,128]{1,0:T(8,128)S(1)} %add_rsqrt_fusion.3, f32[64,128]{1,0:T(8,128)S(1)} %broadcast_multiply_fusion.4), kind=kOutput, calls=%fused_computation.31 | convolution fusion | flops 273678336 | bytes 8487936 | tf_op jit(solution)/shard_map/rsc,cd->rsd/dot_general | solution.py:80
  238.3 16.1 %all-to-all-done.3 = bf16[8,2,65536]{2,1,0:T(2,128)(2,1)S(1)} async-done(((bf16[8,2,65536]{2,1,0:T(2,128)(2,1)}), bf16[8,2,65536]{2,1,0:T(2,128)(2,1)S(1)}, u32[]{:S(2)}, u32[]{:S(2)}) %all-to-all-start.3) | async-done | bytes 2097184 | tf_op jit(solution)/shard_map/all_to_all | solution.py:30
  254.4 5.0 reshape.193
  259.4 4.5 copy.276
  263.9 0.6 copy.316
  264.7 0.5 multiply_reduce_fusion.2
  265.3 0.8 add_convert_fusion.2
  266.1 0.6 copy.281
  266.7 0.7 copy-done.2
  267.4 1.3 copy-done.3
  268.7 2.5 fusion.19
  271.3 0.9 multiply_reduce_fusion.1
  272.2 2.6 convolution_bitcast_fusion
  274.8 3.9 multiply_convert_fusion
  278.7 11.3 %copy.289 = bf16[2,128,64,128]{3,0,2,1:T(2,128)(2,1)} copy(bf16[2,128,64,128]{1,3,0,2:T(8,128)(2,1)} %multiply_convert_fusion) | data formatting | bytes 8388608 | tf_op jit(solution)/shard_map/convert_element_type | solution.py:57
  290.0 54.1 %all_to_all.111 = bf16[2,128,64,128]{3,0,2,1:T(2,128)(2,1)S(1)} all-to-all(bf16[2,128,64,128]{3,0,2,1:T(2,128)(2,1)} %copy.289), channel_id=1, replica_groups=mesh['row'=16,'col'=8] {'row'}, dimensions={1} | all-to-all | bytes 8388608 | tf_op jit(solution)/shard_map/all_to_all | solution.py:18
  344.0 1.1 copy.290
  345.2 1.4 copy.291
  346.9 54.0 %all_to_all.112 = bf16[2,8,1024,128]{3,2,0,1:T(8,128)(2,1)} all-to-all(bf16[2,8,1024,128]{3,2,0,1:T(8,128)(2,1)S(1)} %copy.292), channel_id=1, replica_groups=mesh['row'=16,'col'=8] {'col'}, dimensions={1} | all-to-all | bytes 8388608 | tf_op jit(solution)/shard_map/all_to_all | solution.py:17
  400.9 6.2 %copy.293 = bf16[2,8,1024,128]{2,3,1,0:T(8,128)(2,1)} copy(bf16[2,8,1024,128]{3,2,0,1:T(8,128)(2,1)} %all_to_all.112) | data formatting | bytes 8388608 | tf_op jit(solution)/shard_map/all_to_all | solution.py:17
  407.1 2.7 fusion.17
  409.8 2.4 convert_bitcast_fusion
  412.2 5.2 copy.332
  417.3 12.7 %reduce.21 = bf16[1024,1024]{1,0:T(8,128)(2,1)S(1)} reduce(bf16[1024,1,1024]{2,1,0:T(2,128)(2,1)} %bitcast.168, bf16[]{:T(256)} %broadcast.158), dimensions={1}, to_apply=%bitcast.151.reduce_sub_computation | reduce | bytes 4194306
  430.0 2.8 reshape.194
  432.8 31.6 %all_to_all.113 = bf16[16,2,32768]{2,1,0:T(2,128)(2,1)S(1)} all-to-all(bf16[16,2,32768]{2,1,0:T(2,128)(2,1)} %reshape.194), channel_id=1, replica_groups=mesh['row'=16,'col'=8] {'row'}, dimensions={0} | all-to-all | bytes 4194304 | tf_op jit(solution)/shard_map/all_to_all | solution.py:31
  464.4 6.8 %reshape.195 = bf16[1024,1,1024]{2,1,0:T(2,128)(2,1)} reshape(bf16[16,2,32768]{2,1,0:T(2,128)(2,1)S(1)} %all_to_all.113) | data formatting | bytes 4194304
  471.2 3.0 copy.309
  474.2 4.9 copy.295
  479.1 7.6 %reshape.196 = bf16[8,2,65536]{2,1,0:T(2,128)(2,1)} reshape(bf16[1024,16,64]{2,1,0:T(8,128)(2,1)} %bitcast.173) | data formatting | bytes 4194304
  486.6 3.6 all-to-all-start.7
  490.4 5.1 fusion.11
  495.5 23.0 %all-to-all-done.7 = bf16[8,2,65536]{2,1,0:T(2,128)(2,1)S(1)} async-done(((bf16[8,2,65536]{2,1,0:T(2,128)(2,1)}), bf16[8,2,65536]{2,1,0:T(2,128)(2,1)S(1)}, u32[]{:S(2)}, u32[]{:S(2)}) %all-to-all-start.7) | async-done | bytes 2097184 | tf_op jit(solution)/shard_map/all_to_all | solution.py:30
  518.5 5.0 reshape.197
  523.5 4.5 copy.296
  528.0 0.6 copy.317
  528.8 0.5 multiply_reduce_fusion
  529.3 0.8 add_convert_fusion
  530.2 0.6 copy.297
  530.8 0.7 copy-done.1
  531.5 1.3 copy-done.4
  532.8 4.2 multiply_add_fusion
  537.0 5.6 %copy.300 = f32[64,128,128]{2,1,0:T(8,128)} copy(f32[64,128,128]{1,2,0:T(8,128)} %multiply_add_fusion) | data formatting | bytes 8388608 | tf_op jit(solution)/shard_map/add | solution.py:84
  (38 shorter events, 2.3 us)
Async XLA Ops:
  0.0 7.4 %copy-start.5 = (bf16[2,128,4,128]{3,2,1,0:T(4,128)(2,1)S(1)}, bf16[2,128,4,128]{3,2,1,0:T(4,128)(2,1)}, u32[]{:S(2)}) copy-start(bf16[2,128,4,128]{3,2,1,0:T(4,128)(2,1)} %param.11) | copy-start | bytes 786436
  0.0 8.1 %copy-start.7 = (f32[2,2,128]{2,1,0:T(2,128)S(1)}, f32[2,2,128]{2,1,0:T(2,128)}, u32[]{:S(2)}) copy-start(f32[2,2,128]{2,1,0:T(2,128)} %param.10) | copy-start | bytes 6148
  0.0 8.2 %copy-start.8 = (f32[2,2,128]{2,1,0:T(2,128)S(1)}, f32[2,2,128]{2,1,0:T(2,128)}, u32[]{:S(2)}) copy-start(f32[2,2,128]{2,1,0:T(2,128)} %param.9) | copy-start | bytes 6148
  222.2 32.2 %all-to-all-start.3 = ((bf16[8,2,65536]{2,1,0:T(2,128)(2,1)}), bf16[8,2,65536]{2,1,0:T(2,128)(2,1)S(1)}, u32[]{:S(2)}, u32[]{:S(2)}) async-start(bf16[8,2,65536]{2,1,0:T(2,128)(2,1)} %reshape.192), calls=%async_computation.3 | async-start | bytes 4194304 | tf_op jit(solution)/shard_map/all_to_all | solution.py:30
  226.2 5.8 %copy-start.6 = (bf16[2,128,128]{2,1,0:T(8,128)(2,1)S(1)}, bf16[2,128,128]{2,1,0:T(8,128)(2,1)}, u32[]{:S(2)}) copy-start(bf16[2,128,128]{2,1,0:T(8,128)(2,1)} %param.12) | copy-start | bytes 196612
  265.2 2.2 copy-start.2
  265.2 3.5 copy-start.3
  265.3 3.5 copy-start.9
  271.2 3.6 copy-start
  486.6 31.8 %all-to-all-start.7 = ((bf16[8,2,65536]{2,1,0:T(2,128)(2,1)}), bf16[8,2,65536]{2,1,0:T(2,128)(2,1)S(1)}, u32[]{:S(2)}, u32[]{:S(2)}) async-start(bf16[8,2,65536]{2,1,0:T(2,128)(2,1)} %reshape.196), calls=%async_computation.7 | async-start | bytes 4194304 | tf_op jit(solution)/shard_map/all_to_all | solution.py:30
  529.3 2.2 copy-start.1
  529.3 3.5 copy-start.4
where the time goes:
time: 550 us; the launch traced here: 543 us
  blocking collectives  285 us (52%)
  local copies, waits for them, and re-layouts  135 us (25%)
  other arithmetic  44.5 us (8%)
  waiting for transfers between devices  39 us (7%)
  matrix products  30.3 us (6%)
  starting transfers between devices  7.61 us (1%)
    all_to_all x2, blocking collectives, to_channel_layout(): lax.all_to_all(lax.all_to_all(factors, 'row', split_axis=1, concat_axis=2...  112 us
    all_to_all x2, blocking collectives, to_channel_layout(): lax.all_to_all(factors, 'row', split_axis=1, concat_axis=2, tiled=True)  110 us
    all_to_all x2, blocking collectives, to_tile_layout(): lax.all_to_all(product, 'row', split_axis=1, concat_axis=0, tiled=True)  63 us
    unnamed x34, local copies, waits for them, and re-layouts  61.6 us
    all_to_all x2, waiting for transfers between devices, to_tile_layout(): lax.all_to_all(lax.all_to_all(product, 'row', split_axis=1, concat_axis=0...  39 us
    unnamed x2, other arithmetic  25.4 us
    convert_element_type x2, local copies, waits for them, and re-layouts, per_device(): (jax.nn.sigmoid(projected[1::2]) * projected[0::2] * mask).astype(jnp.bfl...  22.5 us
    dot_general x2, matrix products, per_device(): jnp.einsum('rsc,cd->rsd', normed, gate_weight[layer], preferred_element_t...  11.4 us
  transfers between devices with their start and end apart: 2, of which 2 were waited for; matrix products, arithmetic and copies ran while one was open for 3% of the time, Pallas kernels for 0%

commit v1 on v0

v1 whole, which is shorter than its diff:
```python
import functools

import jax
import jax.numpy as jnp
from jax import lax
from jax.experimental import pallas as pl
from jax.experimental.pallas import tpu as pltpu
from jax.sharding import PartitionSpec as P

epsilon = 1e-05
rows_per_step = 16
mesh_axes = ("row", "col")
vmem_bytes = 48 * 1024 * 1024


def norm_over_channels(values, gain, offset):
    count = values.shape[0]
    centre = jnp.sum(values, axis=0, keepdims=True) * (1.0 / count)
    centred = values - centre
    variance = jnp.sum(centred * centred, axis=0, keepdims=True) * (1.0 / count)
    return centred * lax.rsqrt(variance + epsilon) * gain + offset


def project_pair(normed, row0, weight_ref, mask_args, factor_scratch, n_rows):
    limit, row_base, col_base = mask_args
    channels = weight_ref.shape[1]
    cols = normed.shape[1] // 2
    col_pos = col_base + lax.broadcasted_iota(jnp.int32, (1, cols), 1)
    for side in range(2):
        both = jnp.dot(
            weight_ref[2 * side * channels : 2 * (side + 1) * channels, :],
            normed,
            preferred_element_type=jnp.float32,
        )
        factor = (jnp.tanh(both[channels:]) + 1.0) * both[:channels]
        for t in range(2):
            row = row0 + t
            keep = jnp.logical_and(col_pos < limit, row_base + row < limit).astype(jnp.float32)
            factor_scratch[pl.ds(side * channels * n_rows + row, channels, stride=n_rows), :] = (
                factor[:, t * cols : (t + 1) * cols] * keep
            )


def write_factors(factor_scratch, send_ref):
    channels, sides, n_rows, cols = send_ref.shape
    size = channels * n_rows
    for side in range(sides):
        part = factor_scratch[side * size : (side + 1) * size, :]
        send_ref[:, side] = part.reshape(channels, n_rows, cols).astype(send_ref.dtype)


def mask_positions(place_ref, n_rows):
    return place_ref[0], place_ref[1] + pl.program_id(0) * n_rows, place_ref[2]


def enter_kernel(place_ref, state_ref, weight_ref, affine_ref, send_ref, normed_ref, factor_scratch):
    n_rows = state_ref.shape[0]
    mask_args = mask_positions(place_ref, n_rows)

    def step(pair, carry):
        row0 = pair * 2
        normed = []
        for t in range(2):
            values = state_ref[row0 + t].T
            out = norm_over_channels(values, affine_ref[0], affine_ref[1]).astype(jnp.bfloat16)
            normed_ref[row0 + t] = out
            normed.append(out)
        project_pair(
            jnp.concatenate(normed, axis=1), row0, weight_ref, mask_args, factor_scratch, n_rows
        )
        return carry

    lax.fori_loop(0, n_rows // 2, step, 0)
    write_factors(factor_scratch, send_ref)


def load_returned(returned_ref, product_scratch):
    channels, n_rows, cols = returned_ref.shape
    values = returned_ref[...].astype(jnp.float32)
    product_scratch[...] = values.reshape(channels * n_rows, cols)
    centre = jnp.sum(values, axis=0) * (1.0 / channels)
    centred = product_scratch[...].reshape(channels, n_rows, cols) - centre[None]
    variance = jnp.sum(centred * centred, axis=0) * (1.0 / channels)
    return centre, lax.rsqrt(variance + epsilon)


def update_pair(row0, n_rows, product_scratch, stat_scratch, normed_ref, affine_ref, out_ref, gate_ref):
    channels = out_ref.shape[0]
    hidden = []
    for t in range(2):
        row = row0 + t
        values = product_scratch[pl.ds(row, channels, stride=n_rows), :]
        centre = stat_scratch[0, pl.ds(row, 1), :]
        scale = stat_scratch[1, pl.ds(row, 1), :]
        hidden.append(
            ((values - centre) * scale * affine_ref[2] + affine_ref[3]).astype(jnp.bfloat16)
        )
    term = jnp.dot(
        out_ref[...], jnp.concatenate(hidden, axis=1), preferred_element_type=jnp.float32
    )
    normed = jnp.concatenate([normed_ref[row0], normed_ref[row0 + 1]], axis=1)
    gate = jnp.tanh(jnp.dot(gate_ref[...], normed, preferred_element_type=jnp.float32)) + 1.0
    return gate * term


def middle_kernel(
    place_ref,
    returned_ref,
    state_ref,
    normed_in_ref,
    affine_ref,
    out_weight_ref,
    gate_weight_ref,
    next_weight_ref,
    next_affine_ref,
    send_ref,
    normed_ref,
    new_state_ref,
    factor_scratch,
    product_scratch,
    stat_scratch,
):
    n_rows, channels, cols = new_state_ref.shape
    mask_args = mask_positions(place_ref, n_rows)
    centre, scale = load_returned(returned_ref, product_scratch)
    stat_scratch[0] = centre
    stat_scratch[1] = scale

    def step(pair, carry):
        row0 = pair * 2
        term = update_pair(
            row0,
            n_rows,
            product_scratch,
            stat_scratch,
            normed_in_ref,
            affine_ref,
            out_weight_ref,
            gate_weight_ref,
        )
        normed = []
        for t in range(2):
            values = state_ref[row0 + t].T + term[:, t * cols : (t + 1) * cols]
            new_state_ref[row0 + t] = values
            out = norm_over_channels(values, next_affine_ref[0], next_affine_ref[1])
            out = out.astype(jnp.bfloat16)
            normed_ref[row0 + t] = out
            normed.append(out)
        project_pair(
            jnp.concatenate(normed, axis=1),
            row0,
            next_weight_ref,
            mask_args,
            factor_scratch,
            n_rows,
        )
        return carry

    lax.fori_loop(0, n_rows // 2, step, 0)
    write_factors(factor_scratch, send_ref)


def leave_kernel(
    returned_ref,
    state_ref,
    normed_in_ref,
    affine_ref,
    out_weight_ref,
    gate_weight_ref,
    result_ref,
    product_scratch,
    stat_scratch,
):
    n_rows, cols, channels = result_ref.shape
    centre, scale = load_returned(returned_ref, product_scratch)
    stat_scratch[0] = centre
    stat_scratch[1] = scale

    def step(pair, carry):
        row0 = pair * 2
        term = update_pair(
            row0,
            n_rows,
            product_scratch,
            stat_scratch,
            normed_in_ref,
            affine_ref,
            out_weight_ref,
            gate_weight_ref,
        )
        for t in range(2):
            values = state_ref[row0 + t] + term[:, t * cols : (t + 1) * cols]
            result_ref[row0 + t] = values.T
        return carry

    lax.fori_loop(0, n_rows // 2, step, 0)


def triangle_kernel(n_row, n_col, incoming, left_ref, right_ref, send_ref, left_mat, right_mat):
    tile_rows, tile_cols = left_ref.shape[2:]
    for r in range(n_row):
        for s in range(n_col):
            place = (slice(r * tile_rows, (r + 1) * tile_rows), slice(s * tile_cols, (s + 1) * tile_cols))
            left_mat[place] = left_ref[r * n_col + s, 0]
            right_mat[place] = right_ref[r * n_col + s, 0]
    block = 4 * tile_rows
    for b in range(n_row // 4):
        if incoming:
            product = lax.dot_general(
                left_mat[:, b * block : (b + 1) * block],
                right_mat[...],
                (((0,), (0,)), ((), ())),
                preferred_element_type=jnp.float32,
            )
        else:
            product = lax.dot_general(
                left_mat[b * block : (b + 1) * block, :],
                right_mat[...],
                (((1,), (1,)), ((), ())),
                preferred_element_type=jnp.float32,
            )
        product = product.astype(send_ref.dtype)
        for r in range(4):
            for s in range(n_col):
                send_ref[(b * 4 + r) * n_col + s] = product[
                    r * tile_rows : (r + 1) * tile_rows, s * tile_cols : (s + 1) * tile_cols
                ]


def per_device(pair_map, valid_length, norm_gain, norm_bias, proj_weight, gate_weight, out_weight):
    tile_rows, tile_cols, channels = pair_map.shape
    n_row = lax.axis_size("row")
    n_col = lax.axis_size("col")
    n_dev = n_row * n_col
    n_rows = rows_per_step
    grid = (tile_rows // n_rows,)
    place = jnp.concatenate(
        [
            valid_length,
            jnp.stack([lax.axis_index("row") * tile_rows, lax.axis_index("col") * tile_cols]),
        ]
    ).astype(jnp.int32)
    project = (
        proj_weight.transpose(0, 2, 3, 1).reshape(2, 4 * channels, channels) * jnp.bfloat16(0.5)
    )
    gates = gate_weight.transpose(0, 2, 1) * jnp.bfloat16(0.5)
    outs = out_weight.transpose(0, 2, 1) * jnp.bfloat16(0.5)
    affine = jnp.stack([norm_gain, norm_bias], axis=2).reshape(2, 4, channels, 1)
    affine = jnp.broadcast_to(affine, (2, 4, channels, tile_cols))

    params = pltpu.CompilerParams(
        dimension_semantics=("arbitrary",), vmem_limit_bytes=vmem_bytes
    )
    smem = pl.BlockSpec(memory_space=pltpu.SMEM)

    def whole(array):
        return pl.BlockSpec(array.shape, lambda i: (0,) * array.ndim)

    state_spec = pl.BlockSpec((n_rows, tile_cols, channels), lambda i: (i, 0, 0))
    turned_spec = pl.BlockSpec((n_rows, channels, tile_cols), lambda i: (i, 0, 0))
    send_spec = pl.BlockSpec((channels, 2, n_rows, tile_cols), lambda i: (0, 0, i, 0))
    returned_spec = pl.BlockSpec((channels, n_rows, tile_cols), lambda i: (0, i, 0))
    send_shape = jax.ShapeDtypeStruct((channels, 2, tile_rows, tile_cols), jnp.bfloat16)
    normed_shape = jax.ShapeDtypeStruct((tile_rows, channels, tile_cols), jnp.bfloat16)
    turned_shape = jax.ShapeDtypeStruct((tile_rows, channels, tile_cols), jnp.float32)
    factor_scratch = pltpu.VMEM((2 * channels * n_rows, tile_cols), jnp.float32)
    product_scratch = pltpu.VMEM((channels * n_rows, tile_cols), jnp.float32)
    stat_scratch = pltpu.VMEM((2, n_rows, tile_cols), jnp.float32)

    def exchange(blocks):
        return lax.all_to_all(blocks, mesh_axes, 0, 0, tiled=True)

    def triangle(received, incoming):
        side_spec = lambda side: pl.BlockSpec(
            (n_dev, 1, tile_rows, tile_cols), lambda i: (0, side, 0, 0)
        )
        return pl.pallas_call(
            functools.partial(triangle_kernel, n_row, n_col, incoming),
            grid=(1,),
            out_shape=jax.ShapeDtypeStruct((n_dev, tile_rows, tile_cols), jnp.bfloat16),
            in_specs=[side_spec(0), side_spec(1)],
            out_specs=pl.BlockSpec((n_dev, tile_rows, tile_cols), lambda i: (0, 0, 0)),
            scratch_shapes=[
                pltpu.VMEM((n_row * tile_rows, n_col * tile_cols), jnp.bfloat16),
                pltpu.VMEM((n_row * tile_rows, n_col * tile_cols), jnp.bfloat16),
            ],
            compiler_params=params,
        )(received, received)

    send, normed = pl.pallas_call(
        enter_kernel,
        grid=grid,
        out_shape=[send_shape, normed_shape],
        in_specs=[smem, state_spec, whole(project[0]), whole(affine[0])],
        out_specs=[send_spec, turned_spec],
        scratch_shapes=[factor_scratch],
        compiler_params=params,
    )(place, pair_map, project[0], affine[0])
    returned = exchange(triangle(exchange(send), False))

    send, next_normed, state = pl.pallas_call(
        middle_kernel,
        grid=grid,
        out_shape=[send_shape, normed_shape, turned_shape],
        in_specs=[
            smem,
            returned_spec,
            state_spec,
            turned_spec,
            whole(affine[0]),
            whole(outs[0]),
            whole(gates[0]),
            whole(project[1]),
            whole(affine[1]),
        ],
        out_specs=[send_spec, turned_spec, turned_spec],
        scratch_shapes=[factor_scratch, product_scratch, stat_scratch],
        compiler_params=params,
    )(
        place,
        returned,
        pair_map,
        normed,
        affine[0],
        outs[0],
        gates[0],
        project[1],
        affine[1],
    )
    returned = exchange(triangle(exchange(send), True))

    return pl.pallas_call(
        leave_kernel,
        grid=grid,
        out_shape=jax.ShapeDtypeStruct((tile_rows, tile_cols, channels), jnp.float32),
        in_specs=[
            returned_spec,
            turned_spec,
            turned_spec,
            whole(affine[1]),
            whole(outs[1]),
            whole(gates[1]),
        ],
        out_specs=state_spec,
        scratch_shapes=[product_scratch, stat_scratch],
        compiler_params=params,
    )(returned, state, next_normed, affine[1], outs[1], gates[1])


def solution(mesh):
    placed = (P("row", "col", None), P(), P(), P(), P(), P(), P())
    return jax.shard_map(
        per_device, mesh=mesh, in_specs=placed, out_specs=P("row", "col", None), check_vma=False
    )
```

time: 550 us -> 257 us (0.47); the launches traced: 543 us -> 257 us
  local copies, waits for them, and re-layouts: 135 us -> 3.53 us
  blocking collectives: 285 us -> 155 us
  Pallas kernels: 0 us -> 61.1 us
  other arithmetic: 44.5 us -> 1.89 us
  matrix products: 30.3 us -> 0 us
  waiting for transfers between devices: 39 us -> 28.9 us
    all_to_all x6 -> x3, blocking collectives: 285 us -> 155 us  [exchange(): return lax.all_to_all(blocks, mesh_axes, 0, 0, tiled=True)]
    pallas_call x0 -> x5, Pallas kernels: none -> 61.1 us  [the longest x1 22.3 us: per_device(): pl.pallas_call(middle_kernel, grid=grid, out_shape=[send_shape, normed_sh...]
    unnamed x34 -> x10, local copies, waits for them, and re-layouts: 61.6 us -> 2.89 us
    convert_element_type x6 -> x0, local copies, waits for them, and re-layouts: 34.1 us -> none  [the longest x2 22.5 us: per_device(): (jax.nn.sigmoid(projected[1::2]) * projected[0::2] * mask).astype(jnp.bfl...]
    all_to_all x12 -> x0, local copies, waits for them, and re-layouts: 31 us -> none  [the longest x2 9.73 us: to_tile_layout(): lax.all_to_all(product, 'row', split_axis=1, concat_axis=0, tiled=True)]
    dot_general x8 -> x0, matrix products: 30.3 us -> none  [the longest x2 11.4 us: per_device(): jnp.einsum('rsc,cd->rsd', normed, gate_weight[layer], preferred_element_t...]
    unnamed x2 -> x0, other arithmetic: 25.4 us -> none
    all_to_all x2 -> x1, waiting for transfers between devices: 39 us -> 28.9 us  [exchange(): return lax.all_to_all(blocks, mesh_axes, 0, 0, tiled=True)]
  transfers between devices with their start and end apart: 2 -> 1, of which waited for: 2 -> 1; matrix products, arithmetic and copies ran while one was open for 3% -> 0% of each run, Pallas kernels for 0% -> 0%
where the time goes in v1:
time: 257 us
  blocking collectives  155 us (60%)
  Pallas kernels  61.1 us (24%)
  waiting for transfers between devices  28.9 us (11%)
  starting transfers between devices  5.12 us (2%)
  local copies, waits for them, and re-layouts  3.53 us (1%)
    all_to_all x3, blocking collectives, exchange(): return lax.all_to_all(blocks, mesh_axes, 0, 0, tiled=True)  155 us
    all_to_all x1, waiting for transfers between devices, exchange(): return lax.all_to_all(blocks, mesh_axes, 0, 0, tiled=True)  28.9 us
    pallas_call x1, Pallas kernels, per_device(): pl.pallas_call(middle_kernel, grid=grid, out_shape=[send_shape, normed_sh...  22.3 us
    pallas_call x1, Pallas kernels, per_device(): pl.pallas_call(enter_kernel, grid=grid, out_shape=[send_shape, normed_sha...  16.5 us
    pallas_call x1, Pallas kernels, per_device(): pl.pallas_call(leave_kernel, grid=grid, out_shape=jax.ShapeDtypeStruct((t...  12.8 us
    pallas_call x2, Pallas kernels, triangle(): pl.pallas_call(functools.partial(triangle_kernel, n_row, n_col, incoming)...  9.56 us
  transfers between devices with their start and end apart: 1, of which 1 were waited for; matrix products, arithmetic and copies ran while one was open for 0% of the time, Pallas kernels for 0%

profile of v1, /device:TPU:0, one launch (start us, length us, event | category | flops | bytes accessed | tf_op | source)
XLA Modules:
  0.0 256.8 jit_solution(10974525066202423473)
XLA Ops:
  0.7 0.7 pad_maximum_fusion
  1.4 1.1 multiply_bitcast_fusion
  2.5 0.1 fusion.1
  2.6 0.1 copy.12
  2.7 0.1 pad_add_fusion.place_ref
  2.8 0.1 broadcast_in_dim.12.affine_ref
  2.9 16.5 %shard_map.73 = (bf16[128,2,64,128]{3,2,1,0:T(8,128)(2,1)}, bf16[64,128,128]{2,1,0:T(8,128)(2,1)S(1)}) custom-call(s32[3]{0:T(128)S(1)} %pad_add_fusion.place_ref, f32[64,128,128]{2,1,0:T(8,128)} %state_ref.3, bf16[512,128]{1,0:T(8,128)(2,1)S(1)} %bitcast.23, f32[4,128,128]{2,1,0:T(8,128)S(1)} %broadcast_in_dim.12.affine_ref), custom_call_target="tpu_custom_call" | custom-call | tf_op jit(solution)/shard_map/pallas_call | solution.py:290
  19.4 0.0 copy-start.1
  19.4 1.3 copy-done.1
  20.7 63.3 %all_to_all.20.left_ref.right_ref = bf16[128,2,64,128]{3,2,1,0:T(8,128)(2,1)} all-to-all(bf16[128,2,64,128]{3,2,1,0:T(8,128)(2,1)} %get-tuple-element.10), channel_id=1, replica_groups=mesh['row'=16,'col'=8] {'row','col'}, dimensions={0} | all-to-all | bytes 8388608 | tf_op jit(solution)/shard_map/all_to_all | solution.py:271
  84.1 4.7 %shard_map.74 = bf16[128,64,128]{2,1,0:T(8,128)(2,1)S(1)} custom-call(bf16[128,2,64,128]{3,2,1,0:T(8,128)(2,1)} %all_to_all.20.left_ref.right_ref, bf16[128,2,64,128]{3,2,1,0:T(8,128)(2,1)} %all_to_all.20.left_ref.right_ref), custom_call_target="tpu_custom_call" | custom-call | tf_op jit(solution)/shard_map/pallas_call | solution.py:277
  88.8 0.0 copy-start
  88.8 1.3 copy-done
  90.1 0.0 copy-start.2
  90.1 0.0 copy-start.3
  90.1 5.1 %all-to-all-start.1 = ((bf16[128,64,128]{2,1,0:T(8,128)(2,1)}), bf16[128,64,128]{2,1,0:T(8,128)(2,1)S(1)}, u32[]{:S(2)}, u32[]{:S(2)}) async-start(bf16[128,64,128]{2,1,0:T(8,128)(2,1)} %copy-done), calls=%async_computation.1 | async-start | bytes 4194304 | tf_op jit(solution)/shard_map/all_to_all | solution.py:271
  95.3 0.0 copy-done.2
  95.3 0.1 copy.15
  95.4 0.0 copy-done.3
  95.4 0.1 copy.14
  95.5 0.1 copy.16
  95.7 28.9 %all-to-all-done.1.returned_ref = bf16[128,64,128]{2,1,0:T(8,128)(2,1)S(1)} async-done(((bf16[128,64,128]{2,1,0:T(8,128)(2,1)}), bf16[128,64,128]{2,1,0:T(8,128)(2,1)S(1)}, u32[]{:S(2)}, u32[]{:S(2)}) %all-to-all-start.1) | async-done | bytes 2097184 | tf_op jit(solution)/shard_map/all_to_all | solution.py:271
  124.7 0.1 broadcast_in_dim.14.next_affine_ref.affine_ref
  124.8 22.3 %shard_map.75 = (bf16[128,2,64,128]{3,2,1,0:T(8,128)(2,1)}, bf16[64,128,128]{2,1,0:T(8,128)(2,1)S(1)}, f32[64,128,128]{2,1,0:T(8,128)}) custom-call(s32[3]{0:T(128)S(1)} %pad_add_fusion.place_ref, bf16[128,64,128]{2,1,0:T(8,128)(2,1)S(1)} %all-to-all-done.1.returned_ref, f32[64,128,128]{2,1,0:T(8,128)} %state_ref.3, bf16[64,128,128]{2,1,0:T(8,128)(2,1)} %copy-done.1, ...), custom_call_target="tpu_custom_call" | custom-call | tf_op jit(solution)/shard_map/pallas_call | solution.py:301
  147.1 57.7 %all_to_all.21.left_ref.right_ref = bf16[128,2,64,128]{3,2,1,0:T(8,128)(2,1)} all-to-all(bf16[128,2,64,128]{3,2,1,0:T(8,128)(2,1)} %get-tuple-element.12), channel_id=1, replica_groups=mesh['row'=16,'col'=8] {'row','col'}, dimensions={0} | all-to-all | bytes 8388608 | tf_op jit(solution)/shard_map/all_to_all | solution.py:271
  204.8 4.8 %shard_map.76 = bf16[128,64,128]{2,1,0:T(8,128)(2,1)S(1)} custom-call(bf16[128,2,64,128]{3,2,1,0:T(8,128)(2,1)} %all_to_all.21.left_ref.right_ref, bf16[128,2,64,128]{3,2,1,0:T(8,128)(2,1)} %all_to_all.21.left_ref.right_ref), custom_call_target="tpu_custom_call" | custom-call | tf_op jit(solution)/shard_map/pallas_call | solution.py:277
  209.7 34.3 %all_to_all.22.returned_ref = bf16[128,64,128]{2,1,0:T(8,128)(2,1)S(1)} all-to-all(bf16[128,64,128]{2,1,0:T(8,128)(2,1)S(1)} %shard_map.76), channel_id=1, replica_groups=mesh['row'=16,'col'=8] {'row','col'}, dimensions={0} | all-to-all | bytes 4194304 | tf_op jit(solution)/shard_map/all_to_all | solution.py:271
  244.0 12.8 %shard_map.77 = f32[64,128,128]{2,1,0:T(8,128)} custom-call(bf16[128,64,128]{2,1,0:T(8,128)(2,1)S(1)} %all_to_all.22.returned_ref, f32[64,128,128]{2,1,0:T(8,128)} %get-tuple-element.13.state_ref, bf16[64,128,128]{2,1,0:T(8,128)(2,1)S(1)} %get-tuple-element.14.normed_in_ref, f32[4,128,128]{2,1,0:T(8,128)S(1)} %broadcast_in_dim.14.next_affine_ref.affine_ref, ...), custom_call_target="tpu_custom_call" | custom-call | tf_op jit(solution)/shard_map/pallas_call | solution.py:332
  (5 shorter events, 0.0 us)
Async XLA Ops:
  19.4 1.3 copy-start.1
  88.8 1.3 copy-start
  90.1 5.1 %copy-start.2 = (bf16[2,128,128]{2,1,0:T(8,128)(2,1)S(1)}, bf16[2,128,128]{2,1,0:T(8,128)(2,1)}, u32[]{:S(2)}) copy-start(bf16[2,128,128]{2,1,0:T(8,128)(2,1)} %param.12) | copy-start | bytes 196612
  90.1 5.3 %copy-start.3 = (bf16[2,128,128]{2,1,0:T(8,128)(2,1)S(1)}, bf16[2,128,128]{2,1,0:T(8,128)(2,1)}, u32[]{:S(2)}) copy-start(bf16[2,128,128]{2,1,0:T(8,128)(2,1)} %param.13) | copy-start | bytes 196612
  90.1 34.5 %all-to-all-start.1 = ((bf16[128,64,128]{2,1,0:T(8,128)(2,1)}), bf16[128,64,128]{2,1,0:T(8,128)(2,1)S(1)}, u32[]{:S(2)}, u32[]{:S(2)}) async-start(bf16[128,64,128]{2,1,0:T(8,128)(2,1)} %copy-done), calls=%async_computation.1 | async-start | bytes 4194304 | tf_op jit(solution)/shard_map/all_to_all | solution.py:271

commit v2 on v1

v2 whole, which is shorter than its diff:
```python
import functools

import jax
import jax.numpy as jnp
from jax import lax
from jax.experimental import pallas as pl
from jax.experimental.pallas import tpu as pltpu
from jax.sharding import PartitionSpec as P

epsilon = 1e-05
block_rows = 16
spaced = 24
mesh_axes = ("row", "col")
vmem_bytes = 28 * 1024 * 1024
enter_vmem_bytes = 46 * 1024 * 1024


def norm_over_channels(values, gain, offset):
    count = values.shape[0]
    centre = jnp.sum(values, axis=0, keepdims=True) * (1.0 / count)
    centred = values - centre
    variance = jnp.sum(centred * centred, axis=0, keepdims=True) * (1.0 / count)
    return centred * lax.rsqrt(variance + epsilon) * gain + offset


def project_block(row0, place_ref, normed_ref, weight_ref, send_ref, factor_scratch):
    channels, cols = normed_ref.shape[1:]
    limit, row_base, col_base = place_ref[0], place_ref[1] + row0, place_ref[2]
    col_pos = col_base + lax.broadcasted_iota(jnp.int32, (1, cols), 1)

    def pair(p):
        row = 2 * p
        normed = jnp.concatenate([normed_ref[row0 + row], normed_ref[row0 + row + 1]], axis=1)
        for side in range(2):
            both = jnp.dot(
                weight_ref[2 * side * channels : 2 * (side + 1) * channels, :],
                normed,
                preferred_element_type=jnp.float32,
            )
            factor = (jnp.tanh(both[channels:]) + 1.0) * both[:channels]
            for t in range(2):
                keep = jnp.logical_and(col_pos < limit, row_base + row + t < limit)
                factor_scratch[
                    pl.ds(side * channels * spaced + row + t, channels, stride=spaced), :
                ] = factor[:, t * cols : (t + 1) * cols] * keep.astype(jnp.float32)

    for p in range(block_rows // 2):
        pair(p)
    size = channels * spaced
    for side in range(2):
        part = factor_scratch[side * size : (side + 1) * size, :].reshape(channels, spaced, cols)
        send_ref[:, side, pl.ds(row0, block_rows), :] = part[:, :block_rows].astype(send_ref.dtype)


def update_block(
    row0, returned_ref, normed_ref, affine_ref, out_ref, gate_ref, product_scratch, use_row
):
    channels, cols = normed_ref.shape[1:]
    values = returned_ref[:, pl.ds(row0, block_rows), :].astype(jnp.float32)
    for c in range(channels):
        product_scratch[c * spaced : c * spaced + block_rows, :] = values[c]
    centre = jnp.sum(values, axis=0) * (1.0 / channels)
    variance = jnp.zeros_like(centre)
    for c in range(channels):
        centred = product_scratch[c * spaced : c * spaced + block_rows, :] - centre
        variance = variance + centred * centred
    scale = lax.rsqrt(variance * (1.0 / channels) + epsilon)
    for p in range(block_rows // 2):
        row = 2 * p
        hidden = []
        for t in range(2):
            values = product_scratch[pl.ds(row + t, channels, stride=spaced), :]
            centred = values - centre[row + t : row + t + 1]
            out = centred * scale[row + t : row + t + 1] * affine_ref[2] + affine_ref[3]
            hidden.append(out.astype(jnp.bfloat16))
        term = jnp.dot(
            out_ref[...], jnp.concatenate(hidden, axis=1), preferred_element_type=jnp.float32
        )
        normed = jnp.concatenate([normed_ref[row0 + row], normed_ref[row0 + row + 1]], axis=1)
        gate = jnp.tanh(jnp.dot(gate_ref[...], normed, preferred_element_type=jnp.float32)) + 1.0
        term = gate * term
        for t in range(2):
            use_row(row0 + row + t, term[:, t * cols : (t + 1) * cols])


def over_blocks(n_rows, step):
    def body(b, carry):
        step(b, pl.multiple_of(b * block_rows, block_rows))
        return carry

    lax.fori_loop(0, n_rows // block_rows, body, 0)


def enter_kernel(
    place_ref, state_ref, weight_ref, affine_ref, send_ref, normed_ref, state_buf, sems, factor_scratch
):
    n_rows = state_buf.shape[0]

    def fetch(b):
        rows = pl.ds(b * block_rows, block_rows)
        return pltpu.make_async_copy(state_ref.at[rows], state_buf.at[rows], sems.at[b])

    for b in range(n_rows // block_rows):
        fetch(b).start()

    def step(b, row0):
        fetch(b).wait()
        for t in range(block_rows):
            out = norm_over_channels(state_buf[row0 + t].T, affine_ref[0], affine_ref[1])
            normed_ref[row0 + t] = out.astype(jnp.bfloat16)
        project_block(row0, place_ref, normed_ref, weight_ref, send_ref, factor_scratch)

    over_blocks(n_rows, step)


def middle_kernel(
    place_ref,
    returned_ref,
    state_ref,
    normed_in_ref,
    affine_ref,
    out_weight_ref,
    gate_weight_ref,
    next_weight_ref,
    next_affine_ref,
    send_ref,
    normed_ref,
    new_state_ref,
    factor_scratch,
    product_scratch,
):
    def step(b, row0):
        def use_row(row, term):
            new_state_ref[row] = state_ref[row].T + term

        update_block(
            row0,
            returned_ref,
            normed_in_ref,
            affine_ref,
            out_weight_ref,
            gate_weight_ref,
            product_scratch,
            use_row,
        )
        for t in range(block_rows):
            out = norm_over_channels(
                new_state_ref[row0 + t], next_affine_ref[0], next_affine_ref[1]
            )
            normed_ref[row0 + t] = out.astype(jnp.bfloat16)
        project_block(row0, place_ref, normed_ref, next_weight_ref, send_ref, factor_scratch)

    over_blocks(new_state_ref.shape[0], step)


def leave_kernel(
    returned_ref,
    state_ref,
    normed_in_ref,
    affine_ref,
    out_weight_ref,
    gate_weight_ref,
    result_ref,
    result_buf,
    sems,
    product_scratch,
):
    n_rows = result_buf.shape[0]

    def store(b):
        rows = pl.ds(b * block_rows, block_rows)
        return pltpu.make_async_copy(result_buf.at[rows], result_ref.at[rows], sems.at[b])

    def step(b, row0):
        def use_row(row, term):
            result_buf[row] = (state_ref[row] + term).T

        update_block(
            row0,
            returned_ref,
            normed_in_ref,
            affine_ref,
            out_weight_ref,
            gate_weight_ref,
            product_scratch,
            use_row,
        )
        store(b).start()

    over_blocks(n_rows, step)
    for b in range(n_rows // block_rows):
        store(b).wait()


def triangle_kernel(n_row, n_col, incoming, received_ref, send_ref, left_mat, right_mat):
    tile_rows, tile_cols = received_ref.shape[2:]
    for r in range(n_row):
        for s in range(n_col):
            place = (slice(r * tile_rows, (r + 1) * tile_rows), slice(s * tile_cols, (s + 1) * tile_cols))
            left_mat[place] = received_ref[r * n_col + s, 0]
            right_mat[place] = received_ref[r * n_col + s, 1]
    block = 4 * tile_rows
    for b in range(n_row // 4):
        if incoming:
            product = lax.dot_general(
                left_mat[:, b * block : (b + 1) * block],
                right_mat[...],
                (((0,), (0,)), ((), ())),
                preferred_element_type=jnp.float32,
            )
        else:
            product = lax.dot_general(
                left_mat[b * block : (b + 1) * block, :],
                right_mat[...],
                (((1,), (1,)), ((), ())),
                preferred_element_type=jnp.float32,
            )
        product = product.astype(send_ref.dtype)
        for r in range(4):
            for s in range(n_col):
                send_ref[(b * 4 + r) * n_col + s] = product[
                    r * tile_rows : (r + 1) * tile_rows, s * tile_cols : (s + 1) * tile_cols
                ]


def per_device(pair_map, valid_length, norm_gain, norm_bias, proj_weight, gate_weight, out_weight):
    tile_rows, tile_cols, channels = pair_map.shape
    n_row = lax.axis_size("row")
    n_col = lax.axis_size("col")
    n_dev = n_row * n_col
    place = jnp.concatenate(
        [
            valid_length,
            jnp.stack([lax.axis_index("row") * tile_rows, lax.axis_index("col") * tile_cols]),
        ]
    ).astype(jnp.int32)
    project = (
        proj_weight.transpose(0, 2, 3, 1).reshape(2, 4 * channels, channels) * jnp.bfloat16(0.5)
    )
    gates = gate_weight.transpose(0, 2, 1) * jnp.bfloat16(0.5)
    outs = out_weight.transpose(0, 2, 1) * jnp.bfloat16(0.5)
    affine = jnp.stack([norm_gain, norm_bias], axis=2).reshape(2, 4, channels, 1)
    affine = jnp.broadcast_to(affine, (2, 4, channels, tile_cols))

    params = pltpu.CompilerParams(vmem_limit_bytes=vmem_bytes)
    enter_params = pltpu.CompilerParams(vmem_limit_bytes=enter_vmem_bytes)
    smem = pl.BlockSpec(memory_space=pltpu.SMEM)
    vmem = pl.BlockSpec(memory_space=pltpu.VMEM)
    outside = pl.BlockSpec(memory_space=pltpu.HBM)
    send_shape = jax.ShapeDtypeStruct((channels, 2, tile_rows, tile_cols), jnp.bfloat16)
    normed_shape = jax.ShapeDtypeStruct((tile_rows, channels, tile_cols), jnp.bfloat16)
    turned_shape = jax.ShapeDtypeStruct((tile_rows, channels, tile_cols), jnp.float32)
    state_shape = (tile_rows, tile_cols, channels)
    factor_scratch = pltpu.VMEM((2 * channels * spaced, tile_cols), jnp.float32)
    product_scratch = pltpu.VMEM((channels * spaced, tile_cols), jnp.float32)
    copies = pltpu.SemaphoreType.DMA((tile_rows // block_rows,))

    def exchange(blocks):
        return lax.all_to_all(blocks, mesh_axes, 0, 0, tiled=True)

    def triangle(received, incoming):
        whole = pltpu.VMEM((n_row * tile_rows, n_col * tile_cols), jnp.bfloat16)
        return pl.pallas_call(
            functools.partial(triangle_kernel, n_row, n_col, incoming),
            out_shape=jax.ShapeDtypeStruct((n_dev, tile_rows, tile_cols), jnp.bfloat16),
            in_specs=[vmem],
            out_specs=vmem,
            scratch_shapes=[whole, whole],
            compiler_params=params,
        )(received)

    send, normed = pl.pallas_call(
        enter_kernel,
        out_shape=[send_shape, normed_shape],
        in_specs=[smem, outside, vmem, vmem],
        out_specs=[vmem, vmem],
        scratch_shapes=[pltpu.VMEM(state_shape, jnp.float32), copies, factor_scratch],
        compiler_params=enter_params,
    )(place, pair_map, project[0], affine[0])
    returned = exchange(triangle(exchange(send), False))

    send, next_normed, state = pl.pallas_call(
        middle_kernel,
        out_shape=[send_shape, normed_shape, turned_shape],
        in_specs=[smem] + [vmem] * 8,
        out_specs=[vmem, vmem, vmem],
        scratch_shapes=[factor_scratch, product_scratch],
        compiler_params=params,
    )(
        place,
        returned,
        pair_map,
        normed,
        affine[0],
        outs[0],
        gates[0],
        project[1],
        affine[1],
    )
    returned = exchange(triangle(exchange(send), True))

    return pl.pallas_call(
        leave_kernel,
        out_shape=jax.ShapeDtypeStruct(state_shape, jnp.float32),
        in_specs=[vmem] * 6,
        out_specs=outside,
        scratch_shapes=[pltpu.VMEM(state_shape, jnp.float32), copies, product_scratch],
        compiler_params=params,
    )(returned, state, next_normed, affine[1], outs[1], gates[1])


def solution(mesh):
    placed = (P("row", "col", None), P(), P(), P(), P(), P(), P())
    return jax.shard_map(
        per_device, mesh=mesh, in_specs=placed, out_specs=P("row", "col", None), check_vma=False
    )
```

time: 257 us -> 223 us (0.87)
  Pallas kernels: 61.1 us -> 25.2 us
    pallas_call x3, Pallas kernels: 51.6 us -> 20.1 us  [the longest x1 8.34 us: per_device(): pl.pallas_call(middle_kernel, out_shape=[send_shape, normed_shape, turned...]
    pallas_call x2, Pallas kernels: 9.56 us -> 5.08 us  [triangle(): pl.pallas_call(functools.partial(triangle_kernel, n_row, n_col, incoming)...]
    unnamed x10 -> x14, local copies, waits for them, and re-layouts: 2.89 us -> 5.34 us
where the time goes in v2:
time: 223 us; the launch traced here: 222 us
  blocking collectives  154 us (69%)
  waiting for transfers between devices  28.9 us (13%)
  Pallas kernels  25.2 us (11%)
  local copies, waits for them, and re-layouts  5.98 us (3%)
  starting transfers between devices  5.11 us (2%)
    all_to_all x3, blocking collectives, exchange(): return lax.all_to_all(blocks, mesh_axes, 0, 0, tiled=True)  154 us
    all_to_all x1, waiting for transfers between devices, exchange(): return lax.all_to_all(blocks, mesh_axes, 0, 0, tiled=True)  28.9 us
    pallas_call x1, Pallas kernels, per_device(): pl.pallas_call(middle_kernel, out_shape=[send_shape, normed_shape, turned...  8.34 us
    pallas_call x1, Pallas kernels, per_device(): pl.pallas_call(enter_kernel, out_shape=[send_shape, normed_shape], in_spe...  6.85 us
    unnamed x14, local copies, waits for them, and re-layouts  5.34 us
    all_to_all x1, starting transfers between devices, exchange(): return lax.all_to_all(blocks, mesh_axes, 0, 0, tiled=True)  5.11 us
    pallas_call x2, Pallas kernels, triangle(): pl.pallas_call(functools.partial(triangle_kernel, n_row, n_col, incoming)...  5.08 us
    pallas_call x1, Pallas kernels, per_device(): pl.pallas_call(leave_kernel, out_shape=jax.ShapeDtypeStruct(state_shape,...  4.94 us
  transfers between devices with their start and end apart: 1, of which 1 were waited for; matrix products, arithmetic and copies ran while one was open for 0% of the time, Pallas kernels for 0%

profile of v2, /device:TPU:0, one launch (start us, length us, event | category | flops | bytes accessed | tf_op | source)
XLA Modules:
  0.0 222.2 jit_solution(13456580599592266794)
XLA Ops:
  0.7 0.7 pad_maximum_fusion
  1.4 1.1 multiply_bitcast_fusion
  2.5 0.1 fusion.1
  2.6 0.1 copy.12
  2.7 0.1 pad_add_fusion.place_ref
  2.8 0.1 broadcast_in_dim.12.affine_ref
  2.9 6.9 %shard_map.73 = (bf16[128,2,64,128]{3,2,1,0:T(8,128)(2,1)S(1)}, bf16[64,128,128]{2,1,0:T(8,128)(2,1)S(1)}) custom-call(s32[3]{0:T(128)S(1)} %pad_add_fusion.place_ref, f32[64,128,128]{2,1,0:T(8,128)} %state_ref.3, bf16[512,128]{1,0:T(8,128)(2,1)S(1)} %bitcast.23, f32[4,128,128]{2,1,0:T(8,128)S(1)} %broadcast_in_dim.12.affine_ref), custom_call_target="tpu_custom_call" | custom-call | tf_op jit(solution)/shard_map/pallas_call | solution.py:272
  9.8 0.0 copy-start.2
  9.8 63.0 %all_to_all.20.received_ref = bf16[128,2,64,128]{3,2,1,0:T(8,128)(2,1)S(1)} all-to-all(bf16[128,2,64,128]{3,2,1,0:T(8,128)(2,1)S(1)} %get-tuple-element.10), channel_id=1, replica_groups=mesh['row'=16,'col'=8] {'row','col'}, dimensions={0} | all-to-all | bytes 8388608 | tf_op jit(solution)/shard_map/all_to_all | solution.py:259
  72.8 0.0 copy-done.2
  72.8 0.0 copy-start.4
  72.8 0.0 copy-start.5
  72.8 2.5 %shard_map.74 = bf16[128,64,128]{2,1,0:T(8,128)(2,1)S(1)} custom-call(bf16[128,2,64,128]{3,2,1,0:T(8,128)(2,1)S(1)} %all_to_all.20.received_ref), custom_call_target="tpu_custom_call" | custom-call | tf_op jit(solution)/shard_map/pallas_call | solution.py:263
  75.3 0.0 copy-start.1
  75.3 1.3 copy-done.1
  76.6 5.1 %all-to-all-start.1 = ((bf16[128,64,128]{2,1,0:T(8,128)(2,1)}), bf16[128,64,128]{2,1,0:T(8,128)(2,1)S(1)}, u32[]{:S(2)}, u32[]{:S(2)}) async-start(bf16[128,64,128]{2,1,0:T(8,128)(2,1)} %copy-done.1), calls=%async_computation.1 | async-start | bytes 4194304 | tf_op jit(solution)/shard_map/all_to_all | solution.py:259
  81.7 0.0 copy-done.4
  81.7 0.1 copy.15
  81.9 0.0 copy-done.5
  81.9 0.1 copy.14
  82.0 0.1 copy.16
  82.2 28.9 %all-to-all-done.1.returned_ref = bf16[128,64,128]{2,1,0:T(8,128)(2,1)S(1)} async-done(((bf16[128,64,128]{2,1,0:T(8,128)(2,1)}), bf16[128,64,128]{2,1,0:T(8,128)(2,1)S(1)}, u32[]{:S(2)}, u32[]{:S(2)}) %all-to-all-start.1) | async-done | bytes 2097184 | tf_op jit(solution)/shard_map/all_to_all | solution.py:259
  111.1 0.1 broadcast_in_dim.14.next_affine_ref.affine_ref
  111.3 0.0 copy-start
  111.3 2.2 copy-done
  113.5 0.0 copy-start.3
  113.5 1.6 copy-done.3
  115.1 8.3 %shard_map.75 = (bf16[128,2,64,128]{3,2,1,0:T(8,128)(2,1)S(1)}, bf16[64,128,128]{2,1,0:T(8,128)(2,1)S(1)}, f32[64,128,128]{2,1,0:T(8,128)S(1)}) custom-call(s32[3]{0:T(128)S(1)} %pad_add_fusion.place_ref, bf16[128,64,128]{2,1,0:T(8,128)(2,1)S(1)} %all-to-all-done.1.returned_ref, f32[64,128,128]{2,1,0:T(8,128)S(1)} %copy-done, ...), custom_call_target="tpu_custom_call" | custom-call | tf_op jit(solution)/shard_map/pallas_call | solution.py:282
  123.4 56.8 %all_to_all.21.received_ref = bf16[128,2,64,128]{3,2,1,0:T(8,128)(2,1)S(1)} all-to-all(bf16[128,2,64,128]{3,2,1,0:T(8,128)(2,1)S(1)} %get-tuple-element.12), channel_id=1, replica_groups=mesh['row'=16,'col'=8] {'row','col'}, dimensions={0} | all-to-all | bytes 8388608 | tf_op jit(solution)/shard_map/all_to_all | solution.py:259
  180.3 2.6 %shard_map.76 = bf16[128,64,128]{2,1,0:T(8,128)(2,1)S(1)} custom-call(bf16[128,2,64,128]{3,2,1,0:T(8,128)(2,1)S(1)} %all_to_all.21.received_ref), custom_call_target="tpu_custom_call" | custom-call | tf_op jit(solution)/shard_map/pallas_call | solution.py:263
  182.9 34.3 %all_to_all.22.returned_ref = bf16[128,64,128]{2,1,0:T(8,128)(2,1)S(1)} all-to-all(bf16[128,64,128]{2,1,0:T(8,128)(2,1)S(1)} %shard_map.76), channel_id=1, replica_groups=mesh['row'=16,'col'=8] {'row','col'}, dimensions={0} | all-to-all | bytes 4194304 | tf_op jit(solution)/shard_map/all_to_all | solution.py:259
  217.2 4.9 %shard_map.77 = f32[64,128,128]{2,1,0:T(8,128)} custom-call(bf16[128,64,128]{2,1,0:T(8,128)(2,1)S(1)} %all_to_all.22.returned_ref, f32[64,128,128]{2,1,0:T(8,128)S(1)} %get-tuple-element.13.state_ref, bf16[64,128,128]{2,1,0:T(8,128)(2,1)S(1)} %get-tuple-element.14.normed_in_ref, f32[4,128,128]{2,1,0:T(8,128)S(1)} %broadcast_in_dim.14.next_affine_ref.affine_ref, ...), custom_call_target="tpu_custom_call" | custom-call | tf_op jit(solution)/shard_map/pallas_call | solution.py:302
  (5 shorter events, 0.0 us)
Async XLA Ops:
  9.8 63.0 %copy-start.2 = (bf16[64,128,128]{2,1,0:T(8,128)(2,1)}, bf16[64,128,128]{2,1,0:T(8,128)(2,1)S(1)}, u32[]{:S(2)}) copy-start(bf16[64,128,128]{2,1,0:T(8,128)(2,1)S(1)} %get-tuple-element.11.normed_in_ref) | copy-start | bytes 6291460
  72.8 8.9 %copy-start.4 = (bf16[2,128,128]{2,1,0:T(8,128)(2,1)S(1)}, bf16[2,128,128]{2,1,0:T(8,128)(2,1)}, u32[]{:S(2)}) copy-start(bf16[2,128,128]{2,1,0:T(8,128)(2,1)} %param.12) | copy-start | bytes 196612
  72.8 9.1 %copy-start.5 = (bf16[2,128,128]{2,1,0:T(8,128)(2,1)S(1)}, bf16[2,128,128]{2,1,0:T(8,128)(2,1)}, u32[]{:S(2)}) copy-start(bf16[2,128,128]{2,1,0:T(8,128)(2,1)} %param.13) | copy-start | bytes 196612
  75.3 1.3 copy-start.1
  76.6 34.5 %all-to-all-start.1 = ((bf16[128,64,128]{2,1,0:T(8,128)(2,1)}), bf16[128,64,128]{2,1,0:T(8,128)(2,1)S(1)}, u32[]{:S(2)}, u32[]{:S(2)}) async-start(bf16[128,64,128]{2,1,0:T(8,128)(2,1)} %copy-done.1), calls=%async_computation.1 | async-start | bytes 4194304 | tf_op jit(solution)/shard_map/all_to_all | solution.py:259
  111.3 2.2 copy-start
  113.5 1.6 copy-start.3

commit v3 on v2

--- a/solution.py
+++ b/solution.py
@@ -11,7 +11,7 @@
 block_rows = 16
 spaced = 24
 mesh_axes = ("row", "col")
-vmem_bytes = 28 * 1024 * 1024
+vmem_bytes = 20 * 1024 * 1024
 enter_vmem_bytes = 46 * 1024 * 1024
 
 
@@ -21,6 +21,23 @@
     centred = values - centre
     variance = jnp.sum(centred * centred, axis=0, keepdims=True) * (1.0 / count)
     return centred * lax.rsqrt(variance + epsilon) * gain + offset
+
+
+def turn_weights(layer, place_in, place_out):
+    channels = place_in.shape[1]
+    if len(place_in.shape) == 4:
+        raw = place_in[layer].astype(jnp.float32) * 0.5
+        for g in range(place_in.shape[2]):
+            place_out[g * channels : (g + 1) * channels, :] = raw[:, g, :].T.astype(jnp.bfloat16)
+    else:
+        place_out[...] = (place_in[layer].astype(jnp.float32) * 0.5).T.astype(jnp.bfloat16)
+
+
+def turn_affine(layer, which, gain_ref, bias_ref, affine_ref):
+    channels, cols = affine_ref.shape[1:]
+    for at, ref in enumerate((gain_ref, bias_ref)):
+        line = ref[layer, which : which + 1, :]
+        affine_ref[at] = jnp.broadcast_to(line, (cols, channels)).T
 
 
 def project_block(row0, place_ref, normed_ref, weight_ref, send_ref, factor_scratch):
@@ -71,7 +88,7 @@
         for t in range(2):
             values = product_scratch[pl.ds(row + t, channels, stride=spaced), :]
             centred = values - centre[row + t : row + t + 1]
-            out = centred * scale[row + t : row + t + 1] * affine_ref[2] + affine_ref[3]
+            out = centred * scale[row + t : row + t + 1] * affine_ref[0] + affine_ref[1]
             hidden.append(out.astype(jnp.bfloat16))
         term = jnp.dot(
             out_ref[...], jnp.concatenate(hidden, axis=1), preferred_element_type=jnp.float32
@@ -92,7 +109,18 @@
 
 
 def enter_kernel(
-    place_ref, state_ref, weight_ref, affine_ref, send_ref, normed_ref, state_buf, sems, factor_scratch
+    place_ref,
+    state_ref,
+    project_ref,
+    gain_ref,
+    bias_ref,
+    send_ref,
+    normed_ref,
+    state_buf,
+    sems,
+    factor_scratch,
+    weight_ref,
+    affine_ref,
 ):
     n_rows = state_buf.shape[0]
 
@@ -102,6 +130,8 @@
 
     for b in range(n_rows // block_rows):
         fetch(b).start()
+    turn_weights(0, project_ref, weight_ref)
+    turn_affine(0, 0, gain_ref, bias_ref, affine_ref)
 
     def step(b, row0):
         fetch(b).wait()
@@ -118,17 +148,28 @@
     returned_ref,
     state_ref,
     normed_in_ref,
-    affine_ref,
-    out_weight_ref,
-    gate_weight_ref,
-    next_weight_ref,
-    next_affine_ref,
+    gain_ref,
+    bias_ref,
+    out_ref,
+    gate_ref,
+    project_ref,
     send_ref,
     normed_ref,
     new_state_ref,
     factor_scratch,
     product_scratch,
+    affine_ref,
+    next_affine_ref,
+    out_weight_ref,
+    gate_weight_ref,
+    next_weight_ref,
 ):
+    turn_affine(0, 1, gain_ref, bias_ref, affine_ref)
+    turn_affine(1, 0, gain_ref, bias_ref, next_affine_ref)
+    turn_weights(0, out_ref, out_weight_ref)
+    turn_weights(0, gate_ref, gate_weight_ref)
+    turn_weights(1, project_ref, next_weight_ref)
+
     def step(b, row0):
         def use_row(row, term):
             new_state_ref[row] = state_ref[row].T + term
@@ -157,15 +198,22 @@
     returned_ref,
     state_ref,
     normed_in_ref,
-    affine_ref,
-    out_weight_ref,
-    gate_weight_ref,
+    gain_ref,
+    bias_ref,
+    out_ref,
+    gate_ref,
     result_ref,
     result_buf,
     sems,
     product_scratch,
+    affine_ref,
+    out_weight_ref,
+    gate_weight_ref,
 ):
     n_rows = result_buf.shape[0]
+    turn_affine(1, 1, gain_ref, bias_ref, affine_ref)
+    turn_weights(1, out_ref, out_weight_ref)
+    turn_weights(1, gate_ref, gate_weight_ref)
 
     def store(b):
         rows = pl.ds(b * block_rows, block_rows)
@@ -234,14 +282,6 @@
             jnp.stack([lax.axis_index("row") * tile_rows, lax.axis_index("col") * tile_cols]),
         ]
     ).astype(jnp.int32)
-    project = (
-        proj_weight.transpose(0, 2, 3, 1).reshape(2, 4 * channels, channels) * jnp.bfloat16(0.5)
-    )
-    gates = gate_weight.transpose(0, 2, 1) * jnp.bfloat16(0.5)
-    outs = out_weight.transpose(0, 2, 1) * jnp.bfloat16(0.5)
-    affine = jnp.stack([norm_gain, norm_bias], axis=2).reshape(2, 4, channels, 1)
-    affine = jnp.broadcast_to(affine, (2, 4, channels, tile_cols))
-
     params = pltpu.CompilerParams(vmem_limit_bytes=vmem_bytes)
     enter_params = pltpu.CompilerParams(vmem_limit_bytes=enter_vmem_bytes)
     smem = pl.BlockSpec(memory_space=pltpu.SMEM)
@@ -253,6 +293,9 @@
     state_shape = (tile_rows, tile_cols, channels)
     factor_scratch = pltpu.VMEM((2 * channels * spaced, tile_cols), jnp.float32)
     product_scratch = pltpu.VMEM((channels * spaced, tile_cols), jnp.float32)
+    affine_scratch = pltpu.VMEM((2, channels, tile_cols), jnp.float32)
+    square_scratch = pltpu.VMEM((channels, channels), jnp.bfloat16)
+    project_scratch = pltpu.VMEM((4 * channels, channels), jnp.bfloat16)
     copies = pltpu.SemaphoreType.DMA((tile_rows // block_rows,))
 
     def exchange(blocks):
@@ -272,11 +315,17 @@
     send, normed = pl.pallas_call(
         enter_kernel,
         out_shape=[send_shape, normed_shape],
-        in_specs=[smem, outside, vmem, vmem],
+        in_specs=[smem, outside, vmem, vmem, vmem],
         out_specs=[vmem, vmem],
-        scratch_shapes=[pltpu.VMEM(state_shape, jnp.float32), copies, factor_scratch],
+        scratch_shapes=[
+            pltpu.VMEM(state_shape, jnp.float32),
+            copies,
+            factor_scratch,
+            project_scratch,
+            affine_scratch,
+        ],
         compiler_params=enter_params,
-    )(place, pair_map, project[0], affine[0])
+    )(place, pair_map, proj_weight, norm_gain, norm_bias)
     returned = exchange(triangle(exchange(send), False))
 
     send, next_normed, state = pl.pallas_call(
@@ -284,29 +333,44 @@
         out_shape=[send_shape, normed_shape, turned_shape],
         in_specs=[smem] + [vmem] * 8,
         out_specs=[vmem, vmem, vmem],
-        scratch_shapes=[factor_scratch, product_scratch],
+        scratch_shapes=[
+            factor_scratch,
+            product_scratch,
+            affine_scratch,
+            affine_scratch,
+            square_scratch,
+            square_scratch,
+            project_scratch,
+        ],
         compiler_params=params,
     )(
         place,
         returned,
         pair_map,
         normed,
-        affine[0],
-        outs[0],
-        gates[0],
-        project[1],
-        affine[1],
+        norm_gain,
+        norm_bias,
+        out_weight,
+        gate_weight,
+        proj_weight,
     )
     returned = exchange(triangle(exchange(send), True))
 
     return pl.pallas_call(
         leave_kernel,
         out_shape=jax.ShapeDtypeStruct(state_shape, jnp.float32),
-        in_specs=[vmem] * 6,
+        in_specs=[vmem] * 7,
         out_specs=outside,
-        scratch_shapes=[pltpu.VMEM(state_shape, jnp.float32), copies, product_scratch],
+        scratch_shapes=[
+            pltpu.VMEM(state_shape, jnp.float32),
+            copies,
+            product_scratch,
+            affine_scratch,
+            square_scratch,
+            square_scratch,
+        ],
         compiler_params=params,
-    )(returned, state, next_normed, affine[1], outs[1], gates[1])
+    )(returned, state, next_normed, norm_gain, norm_bias, out_weight, gate_weight)
 
 
 def solution(mesh):

time: 223 us -> 218 us (0.978)
  blocking collectives: 154 us -> 189 us
  waiting for transfers between devices: 28.9 us -> 0 us
  starting transfers between devices: 5.11 us -> 0 us
  local copies, waits for them, and re-layouts: 5.98 us -> 2.32 us
    all_to_all x3 -> x4, blocking collectives: 154 us -> 189 us  [exchange(): return lax.all_to_all(blocks, mesh_axes, 0, 0, tiled=True)]
    all_to_all x1 -> x0, waiting for transfers between devices: 28.9 us -> none  [exchange(): return lax.all_to_all(blocks, mesh_axes, 0, 0, tiled=True)]
    all_to_all x1 -> x0, starting transfers between devices: 5.11 us -> none  [exchange(): return lax.all_to_all(blocks, mesh_axes, 0, 0, tiled=True)]
    unnamed x14 -> x12, local copies, waits for them, and re-layouts: 5.34 us -> 2.32 us
  transfers between devices with their start and end apart: 1 -> 0, of which waited for: 1 -> 0; matrix products, arithmetic and copies ran while one was open for 0% -> 0% of each run, Pallas kernels for 0% -> 0%
where the time goes in v3:
time: 218 us
  blocking collectives  189 us (87%)
  Pallas kernels  26.2 us (12%)
  local copies, waits for them, and re-layouts  2.32 us (1%)
    all_to_all x4, blocking collectives, exchange(): return lax.all_to_all(blocks, mesh_axes, 0, 0, tiled=True)  189 us
    pallas_call x1, Pallas kernels, per_device(): pl.pallas_call(middle_kernel, out_shape=[send_shape, normed_shape, turned...  8.95 us
    pallas_call x1, Pallas kernels, per_device(): pl.pallas_call(enter_kernel, out_shape=[send_shape, normed_shape], in_spe...  7.1 us
    pallas_call x1, Pallas kernels, per_device(): pl.pallas_call(leave_kernel, out_shape=jax.ShapeDtypeStruct(state_shape,...  5.1 us
    pallas_call x2, Pallas kernels, triangle(): pl.pallas_call(functools.partial(triangle_kernel, n_row, n_col, incoming)...  5.08 us

profile of v3, /device:TPU:0, one launch (start us, length us, event | category | flops | bytes accessed | tf_op | source)
XLA Modules:
  0.0 217.9 jit_solution(807510191322864061)
XLA Ops:
  0.7 0.1 pad_add_fusion.place_ref
  0.7 0.0 copy-start.1
  0.7 0.9 copy-done.1
  1.7 0.0 copy-start.4
  1.7 0.7 copy-done.4
  2.4 0.0 copy-start.5
  2.4 0.7 copy-done.5
  3.0 7.1 %shard_map.73 = (bf16[128,2,64,128]{3,2,1,0:T(8,128)(2,1)S(1)}, bf16[64,128,128]{2,1,0:T(8,128)(2,1)S(1)}) custom-call(s32[3]{0:T(128)S(1)} %pad_add_fusion.place_ref, f32[64,128,128]{2,1,0:T(8,128)} %state_ref.3, bf16[2,128,4,128]{3,2,1,0:T(4,128)(2,1)S(1)} %copy-done.1, f32[2,2,128]{2,1,0:T(2,128)S(1)} %copy-done.4, f32[2,2,128]{2,1,0:T(2,128)S(1)} %copy-done.5), custom_call_target="tpu_custom_call" | custom-call | tf_op jit(solution)/shard_map/pallas_call | solution.py:315
  10.2 63.0 %all_to_all.20.received_ref = bf16[128,2,64,128]{3,2,1,0:T(8,128)(2,1)S(1)} all-to-all(bf16[128,2,64,128]{3,2,1,0:T(8,128)(2,1)S(1)} %get-tuple-element.10), channel_id=1, replica_groups=mesh['row'=16,'col'=8] {'row','col'}, dimensions={0} | all-to-all | bytes 8388608 | tf_op jit(solution)/shard_map/all_to_all | solution.py:302
  73.2 0.0 copy-start
  73.2 0.0 copy-start.2
  73.2 0.0 copy-start.3
  73.2 2.5 %shard_map.74 = bf16[128,64,128]{2,1,0:T(8,128)(2,1)S(1)} custom-call(bf16[128,2,64,128]{3,2,1,0:T(8,128)(2,1)S(1)} %all_to_all.20.received_ref), custom_call_target="tpu_custom_call" | custom-call | tf_op jit(solution)/shard_map/pallas_call | solution.py:306
  75.7 34.3 %all_to_all.21.returned_ref = bf16[128,64,128]{2,1,0:T(8,128)(2,1)S(1)} all-to-all(bf16[128,64,128]{2,1,0:T(8,128)(2,1)S(1)} %shard_map.74), channel_id=1, replica_groups=mesh['row'=16,'col'=8] {'row','col'}, dimensions={0} | all-to-all | bytes 4194304 | tf_op jit(solution)/shard_map/all_to_all | solution.py:302
  110.0 0.0 copy-done
  110.0 0.0 copy-done.2
  110.0 0.0 copy-done.3
  110.0 9.0 %shard_map.75 = (bf16[128,2,64,128]{3,2,1,0:T(8,128)(2,1)S(1)}, bf16[64,128,128]{2,1,0:T(8,128)(2,1)S(1)}, f32[64,128,128]{2,1,0:T(8,128)S(1)}) custom-call(s32[3]{0:T(128)S(1)} %pad_add_fusion.place_ref, bf16[128,64,128]{2,1,0:T(8,128)(2,1)S(1)} %all_to_all.21.returned_ref, f32[64,128,128]{2,1,0:T(8,128)S(1)} %copy-done, ...), custom_call_target="tpu_custom_call" | custom-call | tf_op jit(solution)/shard_map/pallas_call | solution.py:331
  119.0 56.8 %all_to_all.22.received_ref = bf16[128,2,64,128]{3,2,1,0:T(8,128)(2,1)S(1)} all-to-all(bf16[128,2,64,128]{3,2,1,0:T(8,128)(2,1)S(1)} %get-tuple-element.12), channel_id=1, replica_groups=mesh['row'=16,'col'=8] {'row','col'}, dimensions={0} | all-to-all | bytes 8388608 | tf_op jit(solution)/shard_map/all_to_all | solution.py:302
  175.8 2.6 %shard_map.76 = bf16[128,64,128]{2,1,0:T(8,128)(2,1)S(1)} custom-call(bf16[128,2,64,128]{3,2,1,0:T(8,128)(2,1)S(1)} %all_to_all.22.received_ref), custom_call_target="tpu_custom_call" | custom-call | tf_op jit(solution)/shard_map/pallas_call | solution.py:306
  178.4 34.3 %all_to_all.23.returned_ref = bf16[128,64,128]{2,1,0:T(8,128)(2,1)S(1)} all-to-all(bf16[128,64,128]{2,1,0:T(8,128)(2,1)S(1)} %shard_map.76), channel_id=1, replica_groups=mesh['row'=16,'col'=8] {'row','col'}, dimensions={0} | all-to-all | bytes 4194304 | tf_op jit(solution)/shard_map/all_to_all | solution.py:302
  212.8 5.1 %shard_map.77 = f32[64,128,128]{2,1,0:T(8,128)} custom-call(bf16[128,64,128]{2,1,0:T(8,128)(2,1)S(1)} %all_to_all.23.returned_ref, f32[64,128,128]{2,1,0:T(8,128)S(1)} %get-tuple-element.13.state_ref, bf16[64,128,128]{2,1,0:T(8,128)(2,1)S(1)} %get-tuple-element.14.normed_in_ref, f32[2,2,128]{2,1,0:T(2,128)S(1)} %copy-done.4, f32[2,2,128]{2,1,0:T(2,128)S(1)} %copy-done.5, ...), custom_call_target="tpu_custom_call" | custom-call | tf_op jit(solution)/shard_map/pallas_call | solution.py:359
Async XLA Ops:
  0.7 1.0 copy-start.1
  1.7 0.7 copy-start.4
  2.4 0.7 copy-start.5
  73.2 36.8 %copy-start = (f32[64,128,128]{2,1,0:T(8,128)S(1)}, f32[64,128,128]{2,1,0:T(8,128)}, u32[]{:S(2)}) copy-start(f32[64,128,128]{2,1,0:T(8,128)} %state_ref.3) | copy-start | bytes 12582916
  73.2 36.8 %copy-start.2 = (bf16[2,128,128]{2,1,0:T(8,128)(2,1)S(1)}, bf16[2,128,128]{2,1,0:T(8,128)(2,1)}, u32[]{:S(2)}) copy-start(bf16[2,128,128]{2,1,0:T(8,128)(2,1)} %out_ref.3) | copy-start | bytes 196612
  73.2 36.8 %copy-start.3 = (bf16[2,128,128]{2,1,0:T(8,128)(2,1)S(1)}, bf16[2,128,128]{2,1,0:T(8,128)(2,1)}, u32[]{:S(2)}) copy-start(bf16[2,128,128]{2,1,0:T(8,128)(2,1)} %gate_ref.3) | copy-start | bytes 196612

commit v4 on v3

v4 whole, which is shorter than its diff:
```python
import functools

import jax
import jax.numpy as jnp
from jax import lax
from jax.experimental import pallas as pl
from jax.experimental.pallas import tpu as pltpu
from jax.sharding import PartitionSpec as P

epsilon = 1e-05
block_rows = 16
pairs_per_block = block_rows // 2
copy_rows = 4
fetch_sizes = (8, 24, 32)
spaced = 24
mesh_axes = ("row", "col")
vmem_bytes = 20 * 1024 * 1024
enter_vmem_bytes = 46 * 1024 * 1024


def norm_over_channels(values, gain, offset):
    count = values.shape[0]
    centre = jnp.sum(values, axis=0, keepdims=True) * (1.0 / count)
    centred = values - centre
    variance = jnp.sum(centred * centred, axis=0, keepdims=True) * (1.0 / count)
    return centred * lax.rsqrt(variance + epsilon) * gain + offset


def turn_weights(layer, place_in, place_out):
    channels = place_in.shape[1]
    if len(place_in.shape) == 4:
        raw = place_in[layer].astype(jnp.float32) * 0.5
        for g in range(place_in.shape[2]):
            place_out[g * channels : (g + 1) * channels, :] = raw[:, g, :].T.astype(jnp.bfloat16)
    else:
        place_out[...] = (place_in[layer].astype(jnp.float32) * 0.5).T.astype(jnp.bfloat16)


def turn_affine(layer, which, gain_ref, bias_ref, affine_ref):
    channels, cols = affine_ref.shape[1:]
    for at, ref in enumerate((gain_ref, bias_ref)):
        line = ref[layer, which : which + 1, :]
        affine_ref[at] = jnp.broadcast_to(line, (cols, channels)).T


def block_pair(row):
    return row // block_rows, row % block_rows


def project_pair(row, place_ref, normed_ref, weight_ref, factor_scratch):
    channels, cols = normed_ref.shape[1:]
    limit, row_base, col_base = place_ref[0], place_ref[1], place_ref[2]
    col_pos = col_base + lax.broadcasted_iota(jnp.int32, (1, cols), 1)
    block, at = block_pair(row)
    normed = jnp.concatenate([normed_ref[row], normed_ref[row + 1]], axis=1)
    for side in range(2):
        both = jnp.dot(
            weight_ref[2 * side * channels : 2 * (side + 1) * channels, :],
            normed,
            preferred_element_type=jnp.float32,
        )
        factor = (jnp.tanh(both[channels:]) + 1.0) * both[:channels]
        for t in range(2):
            keep = jnp.logical_and(col_pos < limit, row_base + row + t < limit)
            first = side * channels * spaced + at + t
            factor_scratch[block % 2, pl.ds(first, channels, stride=spaced), :] = factor[
                :, t * cols : (t + 1) * cols
            ] * keep.astype(jnp.float32)


def write_part(block, part, factor_scratch, send_ref):
    channels, cols = send_ref.shape[0], send_ref.shape[3]
    some = channels // pairs_per_block
    for side in range(2):
        first = (side * channels + part * some) * spaced
        values = factor_scratch[block % 2, first : first + some * spaced, :]
        values = values.reshape(some, spaced, cols)[:, :block_rows].astype(send_ref.dtype)
        rows = slice(block * block_rows, (block + 1) * block_rows)
        send_ref[part * some : (part + 1) * some, side, rows, :] = values


def sum_part(block, part, sums, returned_ref, product_scratch):
    channels = returned_ref.shape[0]
    some = channels // pairs_per_block
    rows = slice(block * block_rows, (block + 1) * block_rows)
    first = returned_ref[0, rows, :].astype(jnp.float32)
    total, squares = sums
    for c in range(part * some, (part + 1) * some):
        values = returned_ref[c, rows, :].astype(jnp.float32)
        product_scratch[block % 2, c * spaced : c * spaced + block_rows, :] = values
        shifted = values - first
        total = total + shifted
        squares = squares + shifted * shifted
    return total, squares


def finish_sums(block, sums, returned_ref, stat_scratch):
    channels = returned_ref.shape[0]
    rows = slice(block * block_rows, (block + 1) * block_rows)
    shift = sums[0] * (1.0 / channels)
    variance = sums[1] * (1.0 / channels) - shift * shift
    stat_scratch[block % 2, 0] = returned_ref[0, rows, :].astype(jnp.float32) + shift
    stat_scratch[block % 2, 1] = lax.rsqrt(jnp.maximum(variance, 0.0) + epsilon)


def update_pair(row, normed_ref, affine_ref, out_ref, gate_ref, product_scratch, stat_scratch):
    channels = normed_ref.shape[1]
    block, at = block_pair(row)
    hidden = []
    for t in range(2):
        values = product_scratch[block % 2, pl.ds(at + t, channels, stride=spaced), :]
        centre = stat_scratch[block % 2, 0, at + t : at + t + 1, :]
        scale = stat_scratch[block % 2, 1, at + t : at + t + 1, :]
        out = (values - centre) * scale * affine_ref[0] + affine_ref[1]
        hidden.append(out.astype(jnp.bfloat16))
    term = jnp.dot(
        out_ref[...], jnp.concatenate(hidden, axis=1), preferred_element_type=jnp.float32
    )
    normed = jnp.concatenate([normed_ref[row], normed_ref[row + 1]], axis=1)
    gate = jnp.tanh(jnp.dot(gate_ref[...], normed, preferred_element_type=jnp.float32)) + 1.0
    return gate * term


def enter_kernel(
    place_ref,
    state_ref,
    early_ref,
    send_ref,
    normed_ref,
    state_buf,
    sems,
    factor_scratch,
    weight_ref,
    affine_ref,
):
    n_rows = state_buf.shape[0]
    n_pairs = n_rows // 2
    n_blocks = n_rows // block_rows
    starts = [sum(fetch_sizes[:b]) for b in range(len(fetch_sizes))]

    def fetch(b):
        rows = pl.ds(starts[b], fetch_sizes[b])
        return pltpu.make_async_copy(state_ref.at[rows], state_buf.at[rows], sems.at[b])

    for b in range(len(starts)):
        fetch(b).start()
    channels = weight_ref.shape[1]
    for g in range(4):
        raw = early_ref[pl.ds(g, channels, stride=4), :] * 0.5
        weight_ref[g * channels : (g + 1) * channels, :] = raw.T.astype(jnp.bfloat16)
    for at in range(2):
        line = early_ref[4 * channels + at : 4 * channels + at + 1, :]
        affine_ref[at] = jnp.broadcast_to(line, (channels, channels)).T

    def normalise(pair):
        if pair < n_pairs:
            for row in (2 * pair, 2 * pair + 1):
                if row in starts:
                    fetch(starts.index(row)).wait()
                out = norm_over_channels(state_buf[row].T, affine_ref[0], affine_ref[1])
                normed_ref[row] = out.astype(jnp.bfloat16)

    normalise(0)
    for block in range(n_blocks + 1):
        for part in range(pairs_per_block):
            pair = block * pairs_per_block + part
            normalise(pair + 1)
            if block < n_blocks:
                project_pair(2 * pair, place_ref, normed_ref, weight_ref, factor_scratch)
            if block > 0:
                write_part(block - 1, part, factor_scratch, send_ref)


def middle_kernel(
    place_ref,
    returned_ref,
    state_ref,
    normed_in_ref,
    gain_ref,
    bias_ref,
    out_ref,
    gate_ref,
    project_ref,
    send_ref,
    normed_ref,
    new_state_ref,
    factor_scratch,
    product_scratch,
    stat_scratch,
    affine_ref,
    next_affine_ref,
    out_weight_ref,
    gate_weight_ref,
    next_weight_ref,
):
    n_rows, channels, cols = new_state_ref.shape
    n_pairs = n_rows // 2
    n_blocks = n_rows // block_rows
    turn_affine(0, 1, gain_ref, bias_ref, affine_ref)
    turn_affine(1, 0, gain_ref, bias_ref, next_affine_ref)
    turn_weights(0, out_ref, out_weight_ref)
    turn_weights(0, gate_ref, gate_weight_ref)
    turn_weights(1, project_ref, next_weight_ref)
    nothing = jnp.zeros((block_rows, cols), jnp.float32)

    def update(pair):
        row = 2 * pair
        term = update_pair(
            row,
            normed_in_ref,
            affine_ref,
            out_weight_ref,
            gate_weight_ref,
            product_scratch,
            stat_scratch,
        )
        for t in range(2):
            values = state_ref[row + t].T + term[:, t * cols : (t + 1) * cols]
            new_state_ref[row + t] = values
            out = norm_over_channels(values, next_affine_ref[0], next_affine_ref[1])
            normed_ref[row + t] = out.astype(jnp.bfloat16)

    for block in range(n_blocks + 3):
        sums = (nothing, nothing)
        for part in range(pairs_per_block):
            if block < n_blocks:
                sums = sum_part(block, part, sums, returned_ref, product_scratch)
            pair = (block - 1) * pairs_per_block + part
            if 0 <= pair < n_pairs:
                update(pair)
            if 0 <= pair - 1 < n_pairs:
                project_pair(
                    2 * (pair - 1), place_ref, normed_ref, next_weight_ref, factor_scratch
                )
            written = (block - 2) * pairs_per_block + part - 1
            if 0 <= written < n_pairs:
                write_part(
                    written // pairs_per_block, written % pairs_per_block, factor_scratch, send_ref
                )
        if block < n_blocks:
            finish_sums(block, sums, returned_ref, stat_scratch)


def leave_kernel(
    returned_ref,
    state_ref,
    normed_in_ref,
    gain_ref,
    bias_ref,
    out_ref,
    gate_ref,
    result_ref,
    result_buf,
    sems,
    product_scratch,
    stat_scratch,
    affine_ref,
    out_weight_ref,
    gate_weight_ref,
):
    n_rows, cols, channels = result_buf.shape
    n_blocks = n_rows // block_rows
    store_rows = n_rows // sems.shape[0]
    turn_affine(1, 1, gain_ref, bias_ref, affine_ref)
    turn_weights(1, out_ref, out_weight_ref)
    turn_weights(1, gate_ref, gate_weight_ref)
    nothing = jnp.zeros((block_rows, cols), jnp.float32)

    def store(b):
        rows = pl.ds(b * store_rows, store_rows)
        return pltpu.make_async_copy(result_buf.at[rows], result_ref.at[rows], sems.at[b])

    for block in range(n_blocks + 1):
        sums = (nothing, nothing)
        for part in range(pairs_per_block):
            if block < n_blocks:
                sums = sum_part(block, part, sums, returned_ref, product_scratch)
            row = 2 * ((block - 1) * pairs_per_block + part)
            if row >= 0:
                term = update_pair(
                    row,
                    normed_in_ref,
                    affine_ref,
                    out_weight_ref,
                    gate_weight_ref,
                    product_scratch,
                    stat_scratch,
                )
                for t in range(2):
                    values = state_ref[row + t] + term[:, t * cols : (t + 1) * cols]
                    result_buf[row + t] = values.T
                if (row + 2) % store_rows == 0:
                    store(row // store_rows).start()
        if block < n_blocks:
            finish_sums(block, sums, returned_ref, stat_scratch)
    for b in range(sems.shape[0]):
        store(b).wait()


def triangle_kernel(n_row, n_col, incoming, received_ref, send_ref, left_mat, right_mat):
    tile_rows, tile_cols = received_ref.shape[2:]
    for r in range(n_row):
        for s in range(n_col):
            place = (slice(r * tile_rows, (r + 1) * tile_rows), slice(s * tile_cols, (s + 1) * tile_cols))
            left_mat[place] = received_ref[r * n_col + s, 0]
            right_mat[place] = received_ref[r * n_col + s, 1]
    block = 4 * tile_rows
    for b in range(n_row // 4):
        if incoming:
            product = lax.dot_general(
                left_mat[:, b * block : (b + 1) * block],
                right_mat[...],
                (((0,), (0,)), ((), ())),
                preferred_element_type=jnp.float32,
            )
        else:
            product = lax.dot_general(
                left_mat[b * block : (b + 1) * block, :],
                right_mat[...],
                (((1,), (1,)), ((), ())),
                preferred_element_type=jnp.float32,
            )
        product = product.astype(send_ref.dtype)
        for r in range(4):
            for s in range(n_col):
                send_ref[(b * 4 + r) * n_col + s] = product[
                    r * tile_rows : (r + 1) * tile_rows, s * tile_cols : (s + 1) * tile_cols
                ]


def per_device(pair_map, valid_length, norm_gain, norm_bias, proj_weight, gate_weight, out_weight):
    tile_rows, tile_cols, channels = pair_map.shape
    n_row = lax.axis_size("row")
    n_col = lax.axis_size("col")
    n_dev = n_row * n_col
    place = jnp.concatenate(
        [
            valid_length,
            jnp.stack([lax.axis_index("row") * tile_rows, lax.axis_index("col") * tile_cols]),
        ]
    ).astype(jnp.int32)
    params = pltpu.CompilerParams(vmem_limit_bytes=vmem_bytes)
    enter_params = pltpu.CompilerParams(vmem_limit_bytes=enter_vmem_bytes)
    smem = pl.BlockSpec(memory_space=pltpu.SMEM)
    vmem = pl.BlockSpec(memory_space=pltpu.VMEM)
    outside = pl.BlockSpec(memory_space=pltpu.HBM)
    send_shape = jax.ShapeDtypeStruct((channels, 2, tile_rows, tile_cols), jnp.bfloat16)
    normed_shape = jax.ShapeDtypeStruct((tile_rows, channels, tile_cols), jnp.bfloat16)
    turned_shape = jax.ShapeDtypeStruct((tile_rows, channels, tile_cols), jnp.float32)
    state_shape = (tile_rows, tile_cols, channels)
    factor_scratch = pltpu.VMEM((2, 2 * channels * spaced, tile_cols), jnp.float32)
    product_scratch = pltpu.VMEM((2, channels * spaced, tile_cols), jnp.float32)
    stat_scratch = pltpu.VMEM((2, 2, block_rows, tile_cols), jnp.float32)
    affine_scratch = pltpu.VMEM((2, channels, tile_cols), jnp.float32)
    square_scratch = pltpu.VMEM((channels, channels), jnp.bfloat16)
    project_scratch = pltpu.VMEM((4 * channels, channels), jnp.bfloat16)
    copies = pltpu.SemaphoreType.DMA((tile_rows // copy_rows,))

    def exchange(blocks):
        return lax.all_to_all(blocks, mesh_axes, 0, 0, tiled=True)

    def triangle(received, incoming):
        whole = pltpu.VMEM((n_row * tile_rows, n_col * tile_cols), jnp.bfloat16)
        return pl.pallas_call(
            functools.partial(triangle_kernel, n_row, n_col, incoming),
            out_shape=jax.ShapeDtypeStruct((n_dev, tile_rows, tile_cols), jnp.bfloat16),
            in_specs=[vmem],
            out_specs=vmem,
            scratch_shapes=[whole, whole],
            compiler_params=params,
        )(received)

    early = jnp.concatenate(
        [
            proj_weight[0].astype(jnp.float32).reshape(4 * channels, channels),
            norm_gain[0, 0:1],
            norm_bias[0, 0:1],
        ]
    )
    send, normed = pl.pallas_call(
        enter_kernel,
        out_shape=[send_shape, normed_shape],
        in_specs=[smem, outside, vmem],
        out_specs=[vmem, vmem],
        scratch_shapes=[
            pltpu.VMEM(state_shape, jnp.float32),
            pltpu.SemaphoreType.DMA((len(fetch_sizes),)),
            factor_scratch,
            project_scratch,
            affine_scratch,
        ],
        compiler_params=enter_params,
    )(place, pair_map, early)
    returned = exchange(triangle(exchange(send), False))

    send, next_normed, state = pl.pallas_call(
        middle_kernel,
        out_shape=[send_shape, normed_shape, turned_shape],
        in_specs=[smem] + [vmem] * 8,
        out_specs=[vmem, vmem, vmem],
        scratch_shapes=[
            factor_scratch,
            product_scratch,
            stat_scratch,
            affine_scratch,
            affine_scratch,
            square_scratch,
            square_scratch,
            project_scratch,
        ],
        compiler_params=params,
    )(
        place,
        returned,
        pair_map,
        normed,
        norm_gain,
        norm_bias,
        out_weight,
        gate_weight,
        proj_weight,
    )
    returned = exchange(triangle(exchange(send), True))

    return pl.pallas_call(
        leave_kernel,
        out_shape=jax.ShapeDtypeStruct(state_shape, jnp.float32),
        in_specs=[vmem] * 7,
        out_specs=outside,
        scratch_shapes=[
            pltpu.VMEM(state_shape, jnp.float32),
            copies,
            product_scratch,
            stat_scratch,
            affine_scratch,
            square_scratch,
            square_scratch,
        ],
        compiler_params=params,
    )(returned, state, next_normed, norm_gain, norm_bias, out_weight, gate_weight)


def solution(mesh):
    placed = (P("row", "col", None), P(), P(), P(), P(), P(), P())
    return jax.shard_map(
        per_device, mesh=mesh, in_specs=placed, out_specs=P("row", "col", None), check_vma=False
    )
```

time: 218 us -> 216 us (level)
    unnamed x12, local copies, waits for them, and re-layouts: 2.32 us -> 0.03 us
where the time goes in v4:
time: 216 us
  blocking collectives  189 us (88%)
  Pallas kernels  24.4 us (11%)
    all_to_all x4, blocking collectives, exchange(): return lax.all_to_all(blocks, mesh_axes, 0, 0, tiled=True)  189 us
    pallas_call x1, Pallas kernels, per_device(): pl.pallas_call(middle_kernel, out_shape=[send_shape, normed_shape, turned...  8.46 us
    pallas_call x1, Pallas kernels, per_device(): pl.pallas_call(enter_kernel, out_shape=[send_shape, normed_shape], in_spe...  6.62 us
    pallas_call x2, Pallas kernels, triangle(): pl.pallas_call(functools.partial(triangle_kernel, n_row, n_col, incoming)...  5.09 us

profile of v4, /device:TPU:0, one launch (start us, length us, event | category | flops | bytes accessed | tf_op | source)
XLA Modules:
  0.0 215.7 jit_solution(9856975261721825086)
XLA Ops:
  0.7 1.0 slice.9
  1.6 0.7 slice_bitcast_fusion
  2.3 0.1 pad_add_fusion.place_ref
  2.4 6.6 %shard_map.73 = (bf16[128,2,64,128]{3,2,1,0:T(8,128)(2,1)S(1)}, bf16[64,128,128]{2,1,0:T(8,128)(2,1)S(1)}) custom-call(s32[3]{0:T(128)S(1)} %pad_add_fusion.place_ref, f32[64,128,128]{2,1,0:T(8,128)} %state_ref.3, f32[514,128]{1,0:T(8,128)S(1)} %pad_maximum_fusion.early_ref), custom_call_target="tpu_custom_call" | custom-call | tf_op jit(solution)/shard_map/pallas_call | solution.py:380
  9.1 63.0 %all_to_all.20.received_ref = bf16[128,2,64,128]{3,2,1,0:T(8,128)(2,1)S(1)} all-to-all(bf16[128,2,64,128]{3,2,1,0:T(8,128)(2,1)S(1)} %get-tuple-element.10), channel_id=1, replica_groups=mesh['row'=16,'col'=8] {'row','col'}, dimensions={0} | all-to-all | bytes 8388608 | tf_op jit(solution)/shard_map/all_to_all | solution.py:360
  72.1 0.0 copy-start
  72.1 0.0 copy-start.1
  72.1 0.0 copy-start.2
  72.1 0.0 copy-start.3
  72.1 0.0 copy-start.4
  72.1 0.0 copy-start.5
  72.1 2.5 %shard_map.74 = bf16[128,64,128]{2,1,0:T(8,128)(2,1)S(1)} custom-call(bf16[128,2,64,128]{3,2,1,0:T(8,128)(2,1)S(1)} %all_to_all.20.received_ref), custom_call_target="tpu_custom_call" | custom-call | tf_op jit(solution)/shard_map/pallas_call | solution.py:364
  74.6 34.3 %all_to_all.21.returned_ref = bf16[128,64,128]{2,1,0:T(8,128)(2,1)S(1)} all-to-all(bf16[128,64,128]{2,1,0:T(8,128)(2,1)S(1)} %shard_map.74), channel_id=1, replica_groups=mesh['row'=16,'col'=8] {'row','col'}, dimensions={0} | all-to-all | bytes 4194304 | tf_op jit(solution)/shard_map/all_to_all | solution.py:360
  108.9 0.0 copy-done
  108.9 0.0 copy-done.1
  109.0 0.0 copy-done.2
  109.0 0.0 copy-done.3
  109.0 0.0 copy-done.4
  109.0 0.0 copy-done.5
  109.0 8.5 %shard_map.75 = (bf16[128,2,64,128]{3,2,1,0:T(8,128)(2,1)S(1)}, bf16[64,128,128]{2,1,0:T(8,128)(2,1)S(1)}, f32[64,128,128]{2,1,0:T(8,128)S(1)}) custom-call(s32[3]{0:T(128)S(1)} %pad_add_fusion.place_ref, bf16[128,64,128]{2,1,0:T(8,128)(2,1)S(1)} %all_to_all.21.returned_ref, f32[64,128,128]{2,1,0:T(8,128)S(1)} %copy-done, ...), custom_call_target="tpu_custom_call" | custom-call | tf_op jit(solution)/shard_map/pallas_call | solution.py:396
  117.5 56.8 %all_to_all.22.received_ref = bf16[128,2,64,128]{3,2,1,0:T(8,128)(2,1)S(1)} all-to-all(bf16[128,2,64,128]{3,2,1,0:T(8,128)(2,1)S(1)} %get-tuple-element.12), channel_id=1, replica_groups=mesh['row'=16,'col'=8] {'row','col'}, dimensions={0} | all-to-all | bytes 8388608 | tf_op jit(solution)/shard_map/all_to_all | solution.py:360
  174.3 2.6 %shard_map.76 = bf16[128,64,128]{2,1,0:T(8,128)(2,1)S(1)} custom-call(bf16[128,2,64,128]{3,2,1,0:T(8,128)(2,1)S(1)} %all_to_all.22.received_ref), custom_call_target="tpu_custom_call" | custom-call | tf_op jit(solution)/shard_map/pallas_call | solution.py:364
  176.9 34.3 %all_to_all.23.returned_ref = bf16[128,64,128]{2,1,0:T(8,128)(2,1)S(1)} all-to-all(bf16[128,64,128]{2,1,0:T(8,128)(2,1)S(1)} %shard_map.76), channel_id=1, replica_groups=mesh['row'=16,'col'=8] {'row','col'}, dimensions={0} | all-to-all | bytes 4194304 | tf_op jit(solution)/shard_map/all_to_all | solution.py:360
  211.3 4.2 %shard_map.77 = f32[64,128,128]{2,1,0:T(8,128)} custom-call(bf16[128,64,128]{2,1,0:T(8,128)(2,1)S(1)} %all_to_all.23.returned_ref, f32[64,128,128]{2,1,0:T(8,128)S(1)} %get-tuple-element.13.state_ref, bf16[64,128,128]{2,1,0:T(8,128)(2,1)S(1)} %get-tuple-element.14.normed_in_ref, f32[2,2,128]{2,1,0:T(2,128)S(1)} %copy-done.5, f32[2,2,128]{2,1,0:T(2,128)S(1)} %copy-done.4, ...), custom_call_target="tpu_custom_call" | custom-call | tf_op jit(solution)/shard_map/pallas_call | solution.py:425
  (2 shorter events, 0.0 us)
Async XLA Ops:
  72.1 36.9 %copy-start = (f32[64,128,128]{2,1,0:T(8,128)S(1)}, f32[64,128,128]{2,1,0:T(8,128)}, u32[]{:S(2)}) copy-start(f32[64,128,128]{2,1,0:T(8,128)} %state_ref.3) | copy-start | bytes 12582916
  72.1 36.9 %copy-start.1 = (bf16[2,128,4,128]{3,2,1,0:T(4,128)(2,1)S(1)}, bf16[2,128,4,128]{3,2,1,0:T(4,128)(2,1)}, u32[]{:S(2)}) copy-start(bf16[2,128,4,128]{3,2,1,0:T(4,128)(2,1)} %project_ref.1) | copy-start | bytes 786436
  72.1 36.9 %copy-start.2 = (bf16[2,128,128]{2,1,0:T(8,128)(2,1)S(1)}, bf16[2,128,128]{2,1,0:T(8,128)(2,1)}, u32[]{:S(2)}) copy-start(bf16[2,128,128]{2,1,0:T(8,128)(2,1)} %out_ref.3) | copy-start | bytes 196612
  72.1 36.9 %copy-start.3 = (bf16[2,128,128]{2,1,0:T(8,128)(2,1)S(1)}, bf16[2,128,128]{2,1,0:T(8,128)(2,1)}, u32[]{:S(2)}) copy-start(bf16[2,128,128]{2,1,0:T(8,128)(2,1)} %gate_ref.3) | copy-start | bytes 196612
  72.1 36.9 %copy-start.4 = (f32[2,2,128]{2,1,0:T(2,128)S(1)}, f32[2,2,128]{2,1,0:T(2,128)}, u32[]{:S(2)}) copy-start(f32[2,2,128]{2,1,0:T(2,128)} %bias_ref.3) | copy-start | bytes 6148
  72.1 36.9 %copy-start.5 = (f32[2,2,128]{2,1,0:T(2,128)S(1)}, f32[2,2,128]{2,1,0:T(2,128)}, u32[]{:S(2)}) copy-start(f32[2,2,128]{2,1,0:T(2,128)} %gain_ref.3) | copy-start | bytes 6148

commit v5 on v4

--- a/solution.py
+++ b/solution.py
@@ -11,8 +11,9 @@
 block_rows = 16
 pairs_per_block = block_rows // 2
 copy_rows = 4
+triangle_parts = 4
 fetch_sizes = (8, 24, 32)
-spaced = 24
+spaced = 18
 mesh_axes = ("row", "col")
 vmem_bytes = 20 * 1024 * 1024
 enter_vmem_bytes = 46 * 1024 * 1024
@@ -52,31 +53,32 @@
     limit, row_base, col_base = place_ref[0], place_ref[1], place_ref[2]
     col_pos = col_base + lax.broadcasted_iota(jnp.int32, (1, cols), 1)
     block, at = block_pair(row)
-    normed = jnp.concatenate([normed_ref[row], normed_ref[row + 1]], axis=1)
+    kept = []
+    for t in range(2):
+        keep = jnp.logical_and(col_pos < limit, row_base + row + t < limit)
+        kept.append(normed_ref[row + t] * keep.astype(jnp.float32).astype(jnp.bfloat16))
     for side in range(2):
-        both = jnp.dot(
-            weight_ref[2 * side * channels : 2 * (side + 1) * channels, :],
-            normed,
-            preferred_element_type=jnp.float32,
-        )
-        factor = (jnp.tanh(both[channels:]) + 1.0) * both[:channels]
         for t in range(2):
-            keep = jnp.logical_and(col_pos < limit, row_base + row + t < limit)
+            both = jnp.dot(
+                weight_ref[2 * side * channels : 2 * (side + 1) * channels, :],
+                kept[t],
+                preferred_element_type=jnp.float32,
+            )
+            factor = (jnp.tanh(both[channels:]) + 1.0) * both[:channels]
             first = side * channels * spaced + at + t
-            factor_scratch[block % 2, pl.ds(first, channels, stride=spaced), :] = factor[
-                :, t * cols : (t + 1) * cols
-            ] * keep.astype(jnp.float32)
+            factor_scratch[block % 2, pl.ds(first, channels, stride=spaced), :] = factor
 
 
 def write_part(block, part, factor_scratch, send_ref):
-    channels, cols = send_ref.shape[0], send_ref.shape[3]
+    channels = send_ref.shape[0]
     some = channels // pairs_per_block
     for side in range(2):
         first = (side * channels + part * some) * spaced
-        values = factor_scratch[block % 2, first : first + some * spaced, :]
-        values = values.reshape(some, spaced, cols)[:, :block_rows].astype(send_ref.dtype)
         rows = slice(block * block_rows, (block + 1) * block_rows)
-        send_ref[part * some : (part + 1) * some, side, rows, :] = values
+        for c in range(some):
+            at = first + c * spaced
+            values = factor_scratch[block % 2, at : at + block_rows, :]
+            send_ref[part * some + c, side, rows, :] = values.astype(send_ref.dtype)
 
 
 def sum_part(block, part, sums, returned_ref, product_scratch):
@@ -299,31 +301,41 @@
 
 def triangle_kernel(n_row, n_col, incoming, received_ref, send_ref, left_mat, right_mat):
     tile_rows, tile_cols = received_ref.shape[2:]
+    n_parts = left_mat.shape[0]
+    part_rows = n_row * tile_rows // n_parts
+
+    def stage(side, r, s, place_ref, row0, col0):
+        place_ref[row0 : row0 + tile_rows, col0 : col0 + tile_cols] = received_ref[
+            r * n_col + s, side
+        ]
+
+    def stage_left(part):
+        place_ref = left_mat.at[part]
+        if incoming:
+            per_part = n_col // n_parts
+            for r in range(n_row):
+                for s in range(per_part):
+                    stage(0, r, part * per_part + s, place_ref, r * tile_rows, s * tile_cols)
+        else:
+            per_part = n_row // n_parts
+            for r in range(per_part):
+                for s in range(n_col):
+                    stage(0, part * per_part + r, s, place_ref, r * tile_rows, s * tile_cols)
+
+    stage_left(0)
     for r in range(n_row):
         for s in range(n_col):
-            place = (slice(r * tile_rows, (r + 1) * tile_rows), slice(s * tile_cols, (s + 1) * tile_cols))
-            left_mat[place] = received_ref[r * n_col + s, 0]
-            right_mat[place] = received_ref[r * n_col + s, 1]
-    block = 4 * tile_rows
-    for b in range(n_row // 4):
-        if incoming:
-            product = lax.dot_general(
-                left_mat[:, b * block : (b + 1) * block],
-                right_mat[...],
-                (((0,), (0,)), ((), ())),
-                preferred_element_type=jnp.float32,
-            )
-        else:
-            product = lax.dot_general(
-                left_mat[b * block : (b + 1) * block, :],
-                right_mat[...],
-                (((1,), (1,)), ((), ())),
-                preferred_element_type=jnp.float32,
-            )
-        product = product.astype(send_ref.dtype)
-        for r in range(4):
+            stage(1, r, s, right_mat, r * tile_rows, s * tile_cols)
+    summed = (((0,), (0,)), ((), ())) if incoming else (((1,), (1,)), ((), ()))
+    for part in range(n_parts):
+        if part + 1 < n_parts:
+            stage_left(part + 1)
+        product = lax.dot_general(
+            left_mat[part], right_mat[...], summed, preferred_element_type=jnp.float32
+        ).astype(send_ref.dtype)
+        for r in range(part_rows // tile_rows):
             for s in range(n_col):
-                send_ref[(b * 4 + r) * n_col + s] = product[
+                send_ref[(part * (part_rows // tile_rows) + r) * n_col + s] = product[
                     r * tile_rows : (r + 1) * tile_rows, s * tile_cols : (s + 1) * tile_cols
                 ]
 
@@ -360,13 +372,18 @@
         return lax.all_to_all(blocks, mesh_axes, 0, 0, tiled=True)
 
     def triangle(received, incoming):
-        whole = pltpu.VMEM((n_row * tile_rows, n_col * tile_cols), jnp.bfloat16)
+        tokens = n_row * tile_rows
+        part = tokens // triangle_parts
+        left_shape = (tokens, part) if incoming else (part, tokens)
         return pl.pallas_call(
             functools.partial(triangle_kernel, n_row, n_col, incoming),
             out_shape=jax.ShapeDtypeStruct((n_dev, tile_rows, tile_cols), jnp.bfloat16),
             in_specs=[vmem],
             out_specs=vmem,
-            scratch_shapes=[whole, whole],
+            scratch_shapes=[
+                pltpu.VMEM((triangle_parts,) + left_shape, jnp.bfloat16),
+                pltpu.VMEM((tokens, tokens), jnp.bfloat16),
+            ],
             compiler_params=params,
         )(received)
 

time: 216 us -> 214 us (level)
  no operation moved by 1% of the time
where the time goes in v5:
time: 214 us
  blocking collectives  189 us (88%)
  Pallas kernels  22.7 us (11%)
    all_to_all x4, blocking collectives, exchange(): return lax.all_to_all(blocks, mesh_axes, 0, 0, tiled=True)  189 us
    pallas_call x1, Pallas kernels, per_device(): pl.pallas_call(middle_kernel, out_shape=[send_shape, normed_shape, turned...  7.71 us
    pallas_call x1, Pallas kernels, per_device(): pl.pallas_call(enter_kernel, out_shape=[send_shape, normed_shape], in_spe...  6.14 us
    pallas_call x2, Pallas kernels, triangle(): pl.pallas_call(functools.partial(triangle_kernel, n_row, n_col, incoming)...  5.07 us

profile of v5, /device:TPU:0, one launch (start us, length us, event | category | flops | bytes accessed | tf_op | source)
XLA Modules:
  0.0 214.0 jit_solution(15821422813754400384)
XLA Ops:
  0.7 1.0 slice.9
  1.6 0.7 slice_bitcast_fusion
  2.3 0.1 pad_add_fusion.place_ref
  2.4 6.1 %shard_map.73 = (bf16[128,2,64,128]{3,2,1,0:T(8,128)(2,1)S(1)}, bf16[64,128,128]{2,1,0:T(8,128)(2,1)S(1)}) custom-call(s32[3]{0:T(128)S(1)} %pad_add_fusion.place_ref, f32[64,128,128]{2,1,0:T(8,128)} %state_ref.3, f32[514,128]{1,0:T(8,128)S(1)} %pad_maximum_fusion.early_ref), custom_call_target="tpu_custom_call" | custom-call | tf_op jit(solution)/shard_map/pallas_call | solution.py:397
  8.6 63.0 %all_to_all.20.received_ref = bf16[128,2,64,128]{3,2,1,0:T(8,128)(2,1)S(1)} all-to-all(bf16[128,2,64,128]{3,2,1,0:T(8,128)(2,1)S(1)} %get-tuple-element.10), channel_id=1, replica_groups=mesh['row'=16,'col'=8] {'row','col'}, dimensions={0} | all-to-all | bytes 8388608 | tf_op jit(solution)/shard_map/all_to_all | solution.py:372
  71.6 0.0 copy-start
  71.6 0.0 copy-start.1
  71.6 0.0 copy-start.2
  71.6 0.0 copy-start.3
  71.6 0.0 copy-start.4
  71.6 0.0 copy-start.5
  71.6 2.5 %shard_map.74 = bf16[128,64,128]{2,1,0:T(8,128)(2,1)S(1)} custom-call(bf16[128,2,64,128]{3,2,1,0:T(8,128)(2,1)S(1)} %all_to_all.20.received_ref), custom_call_target="tpu_custom_call" | custom-call | tf_op jit(solution)/shard_map/pallas_call | solution.py:378
  74.1 34.3 %all_to_all.21.returned_ref = bf16[128,64,128]{2,1,0:T(8,128)(2,1)S(1)} all-to-all(bf16[128,64,128]{2,1,0:T(8,128)(2,1)S(1)} %shard_map.74), channel_id=1, replica_groups=mesh['row'=16,'col'=8] {'row','col'}, dimensions={0} | all-to-all | bytes 4194304 | tf_op jit(solution)/shard_map/all_to_all | solution.py:372
  108.5 0.0 copy-done
  108.5 0.0 copy-done.1
  108.5 0.0 copy-done.2
  108.5 0.0 copy-done.3
  108.5 0.0 copy-done.4
  108.5 0.0 copy-done.5
  108.5 7.7 %shard_map.75 = (bf16[128,2,64,128]{3,2,1,0:T(8,128)(2,1)S(1)}, bf16[64,128,128]{2,1,0:T(8,128)(2,1)S(1)}, f32[64,128,128]{2,1,0:T(8,128)S(1)}) custom-call(s32[3]{0:T(128)S(1)} %pad_add_fusion.place_ref, bf16[128,64,128]{2,1,0:T(8,128)(2,1)S(1)} %all_to_all.21.returned_ref, f32[64,128,128]{2,1,0:T(8,128)S(1)} %copy-done, ...), custom_call_target="tpu_custom_call" | custom-call | tf_op jit(solution)/shard_map/pallas_call | solution.py:413
  116.2 56.8 %all_to_all.22.received_ref = bf16[128,2,64,128]{3,2,1,0:T(8,128)(2,1)S(1)} all-to-all(bf16[128,2,64,128]{3,2,1,0:T(8,128)(2,1)S(1)} %get-tuple-element.12), channel_id=1, replica_groups=mesh['row'=16,'col'=8] {'row','col'}, dimensions={0} | all-to-all | bytes 8388608 | tf_op jit(solution)/shard_map/all_to_all | solution.py:372
  173.1 2.6 %shard_map.76 = bf16[128,64,128]{2,1,0:T(8,128)(2,1)S(1)} custom-call(bf16[128,2,64,128]{3,2,1,0:T(8,128)(2,1)S(1)} %all_to_all.22.received_ref), custom_call_target="tpu_custom_call" | custom-call | tf_op jit(solution)/shard_map/pallas_call | solution.py:378
  175.7 34.3 %all_to_all.23.returned_ref = bf16[128,64,128]{2,1,0:T(8,128)(2,1)S(1)} all-to-all(bf16[128,64,128]{2,1,0:T(8,128)(2,1)S(1)} %shard_map.76), channel_id=1, replica_groups=mesh['row'=16,'col'=8] {'row','col'}, dimensions={0} | all-to-all | bytes 4194304 | tf_op jit(solution)/shard_map/all_to_all | solution.py:372
  210.0 3.8 %shard_map.77 = f32[64,128,128]{2,1,0:T(8,128)} custom-call(bf16[128,64,128]{2,1,0:T(8,128)(2,1)S(1)} %all_to_all.23.returned_ref, f32[64,128,128]{2,1,0:T(8,128)S(1)} %get-tuple-element.13.state_ref, bf16[64,128,128]{2,1,0:T(8,128)(2,1)S(1)} %get-tuple-element.14.normed_in_ref, f32[2,2,128]{2,1,0:T(2,128)S(1)} %copy-done.5, f32[2,2,128]{2,1,0:T(2,128)S(1)} %copy-done.4, ...), custom_call_target="tpu_custom_call" | custom-call | tf_op jit(solution)/shard_map/pallas_call | solution.py:442
  (2 shorter events, 0.0 us)
Async XLA Ops:
  71.6 36.9 %copy-start = (f32[64,128,128]{2,1,0:T(8,128)S(1)}, f32[64,128,128]{2,1,0:T(8,128)}, u32[]{:S(2)}) copy-start(f32[64,128,128]{2,1,0:T(8,128)} %state_ref.3) | copy-start | bytes 12582916
  71.6 36.9 %copy-start.1 = (bf16[2,128,4,128]{3,2,1,0:T(4,128)(2,1)S(1)}, bf16[2,128,4,128]{3,2,1,0:T(4,128)(2,1)}, u32[]{:S(2)}) copy-start(bf16[2,128,4,128]{3,2,1,0:T(4,128)(2,1)} %project_ref.1) | copy-start | bytes 786436
  71.6 36.9 %copy-start.2 = (bf16[2,128,128]{2,1,0:T(8,128)(2,1)S(1)}, bf16[2,128,128]{2,1,0:T(8,128)(2,1)}, u32[]{:S(2)}) copy-start(bf16[2,128,128]{2,1,0:T(8,128)(2,1)} %out_ref.3) | copy-start | bytes 196612
  71.6 36.9 %copy-start.3 = (bf16[2,128,128]{2,1,0:T(8,128)(2,1)S(1)}, bf16[2,128,128]{2,1,0:T(8,128)(2,1)}, u32[]{:S(2)}) copy-start(bf16[2,128,128]{2,1,0:T(8,128)(2,1)} %gate_ref.3) | copy-start | bytes 196612
  71.6 36.9 %copy-start.4 = (f32[2,2,128]{2,1,0:T(2,128)S(1)}, f32[2,2,128]{2,1,0:T(2,128)}, u32[]{:S(2)}) copy-start(f32[2,2,128]{2,1,0:T(2,128)} %bias_ref.3) | copy-start | bytes 6148
  71.6 36.9 %copy-start.5 = (f32[2,2,128]{2,1,0:T(2,128)S(1)}, f32[2,2,128]{2,1,0:T(2,128)}, u32[]{:S(2)}) copy-start(f32[2,2,128]{2,1,0:T(2,128)} %gain_ref.3) | copy-start | bytes 6148

commit v6 on v5

--- a/solution.py
+++ b/solution.py
@@ -12,19 +12,23 @@
 pairs_per_block = block_rows // 2
 copy_rows = 4
 triangle_parts = 4
-fetch_sizes = (8, 24, 32)
+fetch_parts = 4
 spaced = 18
 mesh_axes = ("row", "col")
 vmem_bytes = 20 * 1024 * 1024
-enter_vmem_bytes = 46 * 1024 * 1024
-
-
-def norm_over_channels(values, gain, offset):
+fetch_vmem_bytes = 48 * 1024 * 1024
+
+
+def standardise(values):
     count = values.shape[0]
     centre = jnp.sum(values, axis=0, keepdims=True) * (1.0 / count)
     centred = values - centre
     variance = jnp.sum(centred * centred, axis=0, keepdims=True) * (1.0 / count)
-    return centred * lax.rsqrt(variance + epsilon) * gain + offset
+    return centred * lax.rsqrt(variance + epsilon)
+
+
+def norm_over_channels(values, gain, offset):
+    return standardise(values) * gain + offset
 
 
 def turn_weights(layer, place_in, place_out):
@@ -123,43 +127,44 @@
     return gate * term
 
 
+def fetch_kernel(state_ref, standard_ref, state_buf, sems):
+    n_rows = state_buf.shape[0]
+    fetch_rows = n_rows // sems.shape[0]
+
+    def fetch(b):
+        rows = pl.ds(b * fetch_rows, fetch_rows)
+        return pltpu.make_async_copy(state_ref.at[rows], state_buf.at[rows], sems.at[b])
+
+    for b in range(sems.shape[0]):
+        fetch(b).start()
+    for row in range(n_rows):
+        if row % fetch_rows == 0:
+            fetch(row // fetch_rows).wait()
+        standard_ref[row] = standardise(state_buf[row].T)
+
+
 def enter_kernel(
     place_ref,
-    state_ref,
-    early_ref,
+    standard_ref,
+    project_ref,
+    gain_ref,
+    bias_ref,
     send_ref,
     normed_ref,
-    state_buf,
-    sems,
     factor_scratch,
     weight_ref,
     affine_ref,
 ):
-    n_rows = state_buf.shape[0]
+    n_rows = standard_ref.shape[0]
     n_pairs = n_rows // 2
     n_blocks = n_rows // block_rows
-    starts = [sum(fetch_sizes[:b]) for b in range(len(fetch_sizes))]
-
-    def fetch(b):
-        rows = pl.ds(starts[b], fetch_sizes[b])
-        return pltpu.make_async_copy(state_ref.at[rows], state_buf.at[rows], sems.at[b])
-
-    for b in range(len(starts)):
-        fetch(b).start()
-    channels = weight_ref.shape[1]
-    for g in range(4):
-        raw = early_ref[pl.ds(g, channels, stride=4), :] * 0.5
-        weight_ref[g * channels : (g + 1) * channels, :] = raw.T.astype(jnp.bfloat16)
-    for at in range(2):
-        line = early_ref[4 * channels + at : 4 * channels + at + 1, :]
-        affine_ref[at] = jnp.broadcast_to(line, (channels, channels)).T
+    turn_weights(0, project_ref, weight_ref)
+    turn_affine(0, 0, gain_ref, bias_ref, affine_ref)
 
     def normalise(pair):
         if pair < n_pairs:
             for row in (2 * pair, 2 * pair + 1):
-                if row in starts:
-                    fetch(starts.index(row)).wait()
-                out = norm_over_channels(state_buf[row].T, affine_ref[0], affine_ref[1])
+                out = standard_ref[row] * affine_ref[0] + affine_ref[1]
                 normed_ref[row] = out.astype(jnp.bfloat16)
 
     normalise(0)
@@ -352,7 +357,6 @@
         ]
     ).astype(jnp.int32)
     params = pltpu.CompilerParams(vmem_limit_bytes=vmem_bytes)
-    enter_params = pltpu.CompilerParams(vmem_limit_bytes=enter_vmem_bytes)
     smem = pl.BlockSpec(memory_space=pltpu.SMEM)
     vmem = pl.BlockSpec(memory_space=pltpu.VMEM)
     outside = pl.BlockSpec(memory_space=pltpu.HBM)
@@ -387,27 +391,25 @@
             compiler_params=params,
         )(received)
 
-    early = jnp.concatenate(
-        [
-            proj_weight[0].astype(jnp.float32).reshape(4 * channels, channels),
-            norm_gain[0, 0:1],
-            norm_bias[0, 0:1],
-        ]
-    )
+    standard = pl.pallas_call(
+        fetch_kernel,
+        out_shape=turned_shape,
+        in_specs=[outside],
+        out_specs=vmem,
+        scratch_shapes=[
+            pltpu.VMEM(state_shape, jnp.float32),
+            pltpu.SemaphoreType.DMA((fetch_parts,)),
+        ],
+        compiler_params=pltpu.CompilerParams(vmem_limit_bytes=fetch_vmem_bytes),
+    )(pair_map)
     send, normed = pl.pallas_call(
         enter_kernel,
         out_shape=[send_shape, normed_shape],
-        in_specs=[smem, outside, vmem],
+        in_specs=[smem, vmem, vmem, vmem, vmem],
         out_specs=[vmem, vmem],
-        scratch_shapes=[
-            pltpu.VMEM(state_shape, jnp.float32),
-            pltpu.SemaphoreType.DMA((len(fetch_sizes),)),
-            factor_scratch,
-            project_scratch,
-            affine_scratch,
-        ],
-        compiler_params=enter_params,
-    )(place, pair_map, early)
+        scratch_shapes=[factor_scratch, project_scratch, affine_scratch],
+        compiler_params=params,
+    )(place, standard, proj_weight, norm_gain, norm_bias)
     returned = exchange(triangle(exchange(send), False))
 
     send, next_normed, state = pl.pallas_call(

time: 214 us -> 217 us (1.014)
  local copies, waits for them, and re-layouts: 1.68 us -> 4.21 us
    unnamed x12 -> x16, local copies, waits for them, and re-layouts: 0.03 us -> 4.21 us
    pallas_call x0 -> x1, Pallas kernels: none -> 2.93 us  [per_device(): pl.pallas_call(fetch_kernel, out_shape=turned_shape, in_specs=[outside],...]
    pallas_call x1, Pallas kernels: 6.14 us -> 3.79 us  [per_device(): pl.pallas_call(enter_kernel, out_shape=[send_shape, normed_shape], in_spe...]
where the time goes in v6:
time: 217 us
  blocking collectives  189 us (87%)
  Pallas kernels  23.2 us (11%)
  local copies, waits for them, and re-layouts  4.21 us (2%)
    all_to_all x4, blocking collectives, exchange(): return lax.all_to_all(blocks, mesh_axes, 0, 0, tiled=True)  189 us
    pallas_call x1, Pallas kernels, per_device(): pl.pallas_call(middle_kernel, out_shape=[send_shape, normed_shape, turned...  7.67 us
    pallas_call x2, Pallas kernels, triangle(): pl.pallas_call(functools.partial(triangle_kernel, n_row, n_col, incoming)...  5.07 us

profile of v6, /device:TPU:0, one launch (start us, length us, event | category | flops | bytes accessed | tf_op | source)
XLA Modules:
  0.0 217.0 jit_solution(5750640913396254091)
XLA Ops:
  0.7 0.0 copy-start.3
  0.7 0.0 copy-start.6
  0.7 0.0 copy-start.7
  0.7 2.9 %shard_map.73.standard_ref = f32[64,128,128]{2,1,0:T(8,128)S(1)} custom-call(f32[64,128,128]{2,1,0:T(8,128)} %state_ref.3), custom_call_target="tpu_custom_call" | custom-call | tf_op jit(solution)/shard_map/pallas_call | solution.py:394
  3.6 0.0 copy-start.1
  3.6 2.0 copy-done.1
  5.6 0.1 pad_add_fusion.place_ref
  5.7 0.0 copy-done.3
  5.7 0.0 copy-done.6
  5.7 0.0 copy-done.7
  5.7 0.0 copy-start.2
  5.7 2.2 %copy-done.2 = f32[64,128,128]{2,1,0:T(8,128)S(1)} copy-done((f32[64,128,128]{2,1,0:T(8,128)S(1)}, f32[64,128,128]{2,1,0:T(8,128)}, u32[]{:S(2)}) %copy-start.2) | copy-done | bytes 4194328
  7.9 3.8 %shard_map.74 = (bf16[128,2,64,128]{3,2,1,0:T(8,128)(2,1)S(1)}, bf16[64,128,128]{2,1,0:T(8,128)(2,1)S(1)}) custom-call(s32[3]{0:T(128)S(1)} %pad_add_fusion.place_ref, f32[64,128,128]{2,1,0:T(8,128)S(1)} %copy-done.2, bf16[2,128,4,128]{3,2,1,0:T(4,128)(2,1)S(1)} %copy-done.3, f32[2,2,128]{2,1,0:T(2,128)S(1)} %copy-done.6, f32[2,2,128]{2,1,0:T(2,128)S(1)} %copy-done.7), custom_call_target="tpu_custom_call" | custom-call | tf_op jit(solution)/shard_map/pallas_call | solution.py:405
  11.7 63.0 %all_to_all.20.received_ref = bf16[128,2,64,128]{3,2,1,0:T(8,128)(2,1)S(1)} all-to-all(bf16[128,2,64,128]{3,2,1,0:T(8,128)(2,1)S(1)} %get-tuple-element.10), channel_id=1, replica_groups=mesh['row'=16,'col'=8] {'row','col'}, dimensions={0} | all-to-all | bytes 8388608 | tf_op jit(solution)/shard_map/all_to_all | solution.py:376
  74.7 0.0 copy-start
  74.7 0.0 copy-start.4
  74.7 0.0 copy-start.5
  74.7 2.5 %shard_map.75 = bf16[128,64,128]{2,1,0:T(8,128)(2,1)S(1)} custom-call(bf16[128,2,64,128]{3,2,1,0:T(8,128)(2,1)S(1)} %all_to_all.20.received_ref), custom_call_target="tpu_custom_call" | custom-call | tf_op jit(solution)/shard_map/pallas_call | solution.py:382
  77.2 34.3 %all_to_all.21.returned_ref = bf16[128,64,128]{2,1,0:T(8,128)(2,1)S(1)} all-to-all(bf16[128,64,128]{2,1,0:T(8,128)(2,1)S(1)} %shard_map.75), channel_id=1, replica_groups=mesh['row'=16,'col'=8] {'row','col'}, dimensions={0} | all-to-all | bytes 4194304 | tf_op jit(solution)/shard_map/all_to_all | solution.py:376
  111.6 0.0 copy-done
  111.6 0.0 copy-done.4
  111.6 0.0 copy-done.5
  111.6 7.7 %shard_map.76 = (bf16[128,2,64,128]{3,2,1,0:T(8,128)(2,1)S(1)}, bf16[64,128,128]{2,1,0:T(8,128)(2,1)S(1)}, f32[64,128,128]{2,1,0:T(8,128)S(1)}) custom-call(s32[3]{0:T(128)S(1)} %pad_add_fusion.place_ref, bf16[128,64,128]{2,1,0:T(8,128)(2,1)S(1)} %all_to_all.21.returned_ref, f32[64,128,128]{2,1,0:T(8,128)S(1)} %copy-done, ...), custom_call_target="tpu_custom_call" | custom-call | tf_op jit(solution)/shard_map/pallas_call | solution.py:415
  119.2 56.8 %all_to_all.22.received_ref = bf16[128,2,64,128]{3,2,1,0:T(8,128)(2,1)S(1)} all-to-all(bf16[128,2,64,128]{3,2,1,0:T(8,128)(2,1)S(1)} %get-tuple-element.12), channel_id=1, replica_groups=mesh['row'=16,'col'=8] {'row','col'}, dimensions={0} | all-to-all | bytes 8388608 | tf_op jit(solution)/shard_map/all_to_all | solution.py:376
  176.1 2.6 %shard_map.77 = bf16[128,64,128]{2,1,0:T(8,128)(2,1)S(1)} custom-call(bf16[128,2,64,128]{3,2,1,0:T(8,128)(2,1)S(1)} %all_to_all.22.received_ref), custom_call_target="tpu_custom_call" | custom-call | tf_op jit(solution)/shard_map/pallas_call | solution.py:382
  178.7 34.3 %all_to_all.23.returned_ref = bf16[128,64,128]{2,1,0:T(8,128)(2,1)S(1)} all-to-all(bf16[128,64,128]{2,1,0:T(8,128)(2,1)S(1)} %shard_map.77), channel_id=1, replica_groups=mesh['row'=16,'col'=8] {'row','col'}, dimensions={0} | all-to-all | bytes 4194304 | tf_op jit(solution)/shard_map/all_to_all | solution.py:376
  213.0 3.8 %shard_map.78 = f32[64,128,128]{2,1,0:T(8,128)} custom-call(bf16[128,64,128]{2,1,0:T(8,128)(2,1)S(1)} %all_to_all.23.returned_ref, f32[64,128,128]{2,1,0:T(8,128)S(1)} %get-tuple-element.13.state_ref, bf16[64,128,128]{2,1,0:T(8,128)(2,1)S(1)} %get-tuple-element.14.normed_in_ref, f32[2,2,128]{2,1,0:T(2,128)S(1)} %copy-done.6, f32[2,2,128]{2,1,0:T(2,128)S(1)} %copy-done.7, ...), custom_call_target="tpu_custom_call" | custom-call | tf_op jit(solution)/shard_map/pallas_call | solution.py:444
Async XLA Ops:
  0.7 5.1 %copy-start.3 = (bf16[2,128,4,128]{3,2,1,0:T(4,128)(2,1)S(1)}, bf16[2,128,4,128]{3,2,1,0:T(4,128)(2,1)}, u32[]{:S(2)}) copy-start(bf16[2,128,4,128]{3,2,1,0:T(4,128)(2,1)} %project_ref.3) | copy-start | bytes 786436
  0.7 5.1 %copy-start.6 = (f32[2,2,128]{2,1,0:T(2,128)S(1)}, f32[2,2,128]{2,1,0:T(2,128)}, u32[]{:S(2)}) copy-start(f32[2,2,128]{2,1,0:T(2,128)} %gain_ref.5) | copy-start | bytes 6148
  0.7 5.0 %copy-start.7 = (f32[2,2,128]{2,1,0:T(2,128)S(1)}, f32[2,2,128]{2,1,0:T(2,128)}, u32[]{:S(2)}) copy-start(f32[2,2,128]{2,1,0:T(2,128)} %bias_ref.5) | copy-start | bytes 6148
  3.6 2.0 copy-start.1
  5.7 2.2 %copy-start.2 = (f32[64,128,128]{2,1,0:T(8,128)S(1)}, f32[64,128,128]{2,1,0:T(8,128)}, u32[]{:S(2)}) copy-start(f32[64,128,128]{2,1,0:T(8,128)} %copy-done.1) | copy-start | bytes 12582916
  74.7 36.8 %copy-start = (f32[64,128,128]{2,1,0:T(8,128)S(1)}, f32[64,128,128]{2,1,0:T(8,128)}, u32[]{:S(2)}) copy-start(f32[64,128,128]{2,1,0:T(8,128)} %state_ref.3) | copy-start | bytes 12582916
  74.7 36.8 %copy-start.4 = (bf16[2,128,128]{2,1,0:T(8,128)(2,1)S(1)}, bf16[2,128,128]{2,1,0:T(8,128)(2,1)}, u32[]{:S(2)}) copy-start(bf16[2,128,128]{2,1,0:T(8,128)(2,1)} %out_ref.3) | copy-start | bytes 196612
  74.7 36.8 %copy-start.5 = (bf16[2,128,128]{2,1,0:T(8,128)(2,1)S(1)}, bf16[2,128,128]{2,1,0:T(8,128)(2,1)}, u32[]{:S(2)}) copy-start(bf16[2,128,128]{2,1,0:T(8,128)(2,1)} %gate_ref.3) | copy-start | bytes 196612

commit v7 on v6

--- a/solution.py
+++ b/solution.py
@@ -127,7 +127,7 @@
     return gate * term
 
 
-def fetch_kernel(state_ref, standard_ref, state_buf, sems):
+def fetch_kernel(place_ref, state_ref, standard_ref, state_buf, sems):
     n_rows = state_buf.shape[0]
     fetch_rows = n_rows // sems.shape[0]
 
@@ -394,14 +394,14 @@
     standard = pl.pallas_call(
         fetch_kernel,
         out_shape=turned_shape,
-        in_specs=[outside],
+        in_specs=[smem, outside],
         out_specs=vmem,
         scratch_shapes=[
             pltpu.VMEM(state_shape, jnp.float32),
             pltpu.SemaphoreType.DMA((fetch_parts,)),
         ],
         compiler_params=pltpu.CompilerParams(vmem_limit_bytes=fetch_vmem_bytes),
-    )(pair_map)
+    )(place, pair_map)
     send, normed = pl.pallas_call(
         enter_kernel,
         out_shape=[send_shape, normed_shape],

time: 217 us -> 214 us (0.986)
  local copies, waits for them, and re-layouts: 4.21 us -> 0.02 us
    unnamed x16 -> x12, local copies, waits for them, and re-layouts: 4.21 us -> 0.02 us
where the time goes in v7:
time: 214 us; the launch traced here: 213 us
  blocking collectives  189 us (88%)
  Pallas kernels  23.9 us (11%)
    all_to_all x4, blocking collectives, exchange(): return lax.all_to_all(blocks, mesh_axes, 0, 0, tiled=True)  189 us
    pallas_call x1, Pallas kernels, per_device(): pl.pallas_call(middle_kernel, out_shape=[send_shape, normed_shape, turned...  7.67 us
    pallas_call x2, Pallas kernels, triangle(): pl.pallas_call(functools.partial(triangle_kernel, n_row, n_col, incoming)...  5.07 us

profile of v7, /device:TPU:0, one launch (start us, length us, event | category | flops | bytes accessed | tf_op | source)
XLA Modules:
  0.0 213.4 jit_solution(14823066491157153023)
XLA Ops:
  0.7 0.1 pad_add_fusion.place_ref
  0.7 0.0 copy-start.1
  0.7 0.0 copy-start.4
  0.7 0.0 copy-start.5
  0.7 3.4 %shard_map.73.standard_ref = f32[64,128,128]{2,1,0:T(8,128)S(1)} custom-call(s32[3]{0:T(128)S(1)} %pad_add_fusion.place_ref, f32[64,128,128]{2,1,0:T(8,128)} %state_ref.3), custom_call_target="tpu_custom_call" | custom-call | tf_op jit(solution)/shard_map/pallas_call | solution.py:394
  4.2 0.0 copy-done.1
  4.2 0.0 copy-done.4
  4.2 0.0 copy-done.5
  4.2 3.9 %shard_map.74 = (bf16[128,2,64,128]{3,2,1,0:T(8,128)(2,1)S(1)}, bf16[64,128,128]{2,1,0:T(8,128)(2,1)S(1)}) custom-call(s32[3]{0:T(128)S(1)} %pad_add_fusion.place_ref, f32[64,128,128]{2,1,0:T(8,128)S(1)} %shard_map.73.standard_ref, bf16[2,128,4,128]{3,2,1,0:T(4,128)(2,1)S(1)} %copy-done.1, f32[2,2,128]{2,1,0:T(2,128)S(1)} %copy-done.4, ...), custom_call_target="tpu_custom_call" | custom-call | tf_op jit(solution)/shard_map/pallas_call | solution.py:405
  8.1 63.0 %all_to_all.20.received_ref = bf16[128,2,64,128]{3,2,1,0:T(8,128)(2,1)S(1)} all-to-all(bf16[128,2,64,128]{3,2,1,0:T(8,128)(2,1)S(1)} %get-tuple-element.10), channel_id=1, replica_groups=mesh['row'=16,'col'=8] {'row','col'}, dimensions={0} | all-to-all | bytes 8388608 | tf_op jit(solution)/shard_map/all_to_all | solution.py:376
  71.1 0.0 copy-start
  71.1 0.0 copy-start.2
  71.1 0.0 copy-start.3
  71.1 2.5 %shard_map.75 = bf16[128,64,128]{2,1,0:T(8,128)(2,1)S(1)} custom-call(bf16[128,2,64,128]{3,2,1,0:T(8,128)(2,1)S(1)} %all_to_all.20.received_ref), custom_call_target="tpu_custom_call" | custom-call | tf_op jit(solution)/shard_map/pallas_call | solution.py:382
  73.6 34.3 %all_to_all.21.returned_ref = bf16[128,64,128]{2,1,0:T(8,128)(2,1)S(1)} all-to-all(bf16[128,64,128]{2,1,0:T(8,128)(2,1)S(1)} %shard_map.75), channel_id=1, replica_groups=mesh['row'=16,'col'=8] {'row','col'}, dimensions={0} | all-to-all | bytes 4194304 | tf_op jit(solution)/shard_map/all_to_all | solution.py:376
  108.0 0.0 copy-done
  108.0 0.0 copy-done.2
  108.0 0.0 copy-done.3
  108.0 7.7 %shard_map.76 = (bf16[128,2,64,128]{3,2,1,0:T(8,128)(2,1)S(1)}, bf16[64,128,128]{2,1,0:T(8,128)(2,1)S(1)}, f32[64,128,128]{2,1,0:T(8,128)S(1)}) custom-call(s32[3]{0:T(128)S(1)} %pad_add_fusion.place_ref, bf16[128,64,128]{2,1,0:T(8,128)(2,1)S(1)} %all_to_all.21.returned_ref, f32[64,128,128]{2,1,0:T(8,128)S(1)} %copy-done, ...), custom_call_target="tpu_custom_call" | custom-call | tf_op jit(solution)/shard_map/pallas_call | solution.py:415
  115.6 56.8 %all_to_all.22.received_ref = bf16[128,2,64,128]{3,2,1,0:T(8,128)(2,1)S(1)} all-to-all(bf16[128,2,64,128]{3,2,1,0:T(8,128)(2,1)S(1)} %get-tuple-element.12), channel_id=1, replica_groups=mesh['row'=16,'col'=8] {'row','col'}, dimensions={0} | all-to-all | bytes 8388608 | tf_op jit(solution)/shard_map/all_to_all | solution.py:376
  172.5 2.6 %shard_map.77 = bf16[128,64,128]{2,1,0:T(8,128)(2,1)S(1)} custom-call(bf16[128,2,64,128]{3,2,1,0:T(8,128)(2,1)S(1)} %all_to_all.22.received_ref), custom_call_target="tpu_custom_call" | custom-call | tf_op jit(solution)/shard_map/pallas_call | solution.py:382
  175.1 34.3 %all_to_all.23.returned_ref = bf16[128,64,128]{2,1,0:T(8,128)(2,1)S(1)} all-to-all(bf16[128,64,128]{2,1,0:T(8,128)(2,1)S(1)} %shard_map.77), channel_id=1, replica_groups=mesh['row'=16,'col'=8] {'row','col'}, dimensions={0} | all-to-all | bytes 4194304 | tf_op jit(solution)/shard_map/all_to_all | solution.py:376
  209.4 3.8 %shard_map.78 = f32[64,128,128]{2,1,0:T(8,128)} custom-call(bf16[128,64,128]{2,1,0:T(8,128)(2,1)S(1)} %all_to_all.23.returned_ref, f32[64,128,128]{2,1,0:T(8,128)S(1)} %get-tuple-element.13.state_ref, bf16[64,128,128]{2,1,0:T(8,128)(2,1)S(1)} %get-tuple-element.14.normed_in_ref, f32[2,2,128]{2,1,0:T(2,128)S(1)} %copy-done.4, f32[2,2,128]{2,1,0:T(2,128)S(1)} %copy-done.5, ...), custom_call_target="tpu_custom_call" | custom-call | tf_op jit(solution)/shard_map/pallas_call | solution.py:444
Async XLA Ops:
  0.7 3.4 %copy-start.1 = (bf16[2,128,4,128]{3,2,1,0:T(4,128)(2,1)S(1)}, bf16[2,128,4,128]{3,2,1,0:T(4,128)(2,1)}, u32[]{:S(2)}) copy-start(bf16[2,128,4,128]{3,2,1,0:T(4,128)(2,1)} %project_ref.3) | copy-start | bytes 786436
  0.7 3.5 %copy-start.4 = (f32[2,2,128]{2,1,0:T(2,128)S(1)}, f32[2,2,128]{2,1,0:T(2,128)}, u32[]{:S(2)}) copy-start(f32[2,2,128]{2,1,0:T(2,128)} %gain_ref.5) | copy-start | bytes 6148
  0.7 3.5 %copy-start.5 = (f32[2,2,128]{2,1,0:T(2,128)S(1)}, f32[2,2,128]{2,1,0:T(2,128)}, u32[]{:S(2)}) copy-start(f32[2,2,128]{2,1,0:T(2,128)} %bias_ref.5) | copy-start | bytes 6148
  71.1 36.8 %copy-start = (f32[64,128,128]{2,1,0:T(8,128)S(1)}, f32[64,128,128]{2,1,0:T(8,128)}, u32[]{:S(2)}) copy-start(f32[64,128,128]{2,1,0:T(8,128)} %state_ref.3) | copy-start | bytes 12582916
  71.1 36.8 %copy-start.2 = (bf16[2,128,128]{2,1,0:T(8,128)(2,1)S(1)}, bf16[2,128,128]{2,1,0:T(8,128)(2,1)}, u32[]{:S(2)}) copy-start(bf16[2,128,128]{2,1,0:T(8,128)(2,1)} %out_ref.3) | copy-start | bytes 196612
  71.1 36.8 %copy-start.3 = (bf16[2,128,128]{2,1,0:T(8,128)(2,1)S(1)}, bf16[2,128,128]{2,1,0:T(8,128)(2,1)}, u32[]{:S(2)}) copy-start(bf16[2,128,128]{2,1,0:T(8,128)(2,1)} %gate_ref.3) | copy-start | bytes 196612

commit v8 on v7

--- a/solution.py
+++ b/solution.py
@@ -364,8 +364,8 @@
     normed_shape = jax.ShapeDtypeStruct((tile_rows, channels, tile_cols), jnp.bfloat16)
     turned_shape = jax.ShapeDtypeStruct((tile_rows, channels, tile_cols), jnp.float32)
     state_shape = (tile_rows, tile_cols, channels)
-    factor_scratch = pltpu.VMEM((2, 2 * channels * spaced, tile_cols), jnp.float32)
-    product_scratch = pltpu.VMEM((2, channels * spaced, tile_cols), jnp.float32)
+    factor_scratch = pltpu.VMEM((2, (2 * channels + 1) * spaced, tile_cols), jnp.float32)
+    product_scratch = pltpu.VMEM((2, (channels + 1) * spaced, tile_cols), jnp.float32)
     stat_scratch = pltpu.VMEM((2, 2, block_rows, tile_cols), jnp.float32)
     affine_scratch = pltpu.VMEM((2, channels, tile_cols), jnp.float32)
     square_scratch = pltpu.VMEM((channels, channels), jnp.bfloat16)

time: 214 us -> 214 us (level)
  no operation moved by 1% of the time
where the time goes in v8:
time: 214 us; the launch traced here: 213 us
  blocking collectives  189 us (88%)
  Pallas kernels  23.8 us (11%)
    all_to_all x4, blocking collectives, exchange(): return lax.all_to_all(blocks, mesh_axes, 0, 0, tiled=True)  189 us
    pallas_call x1, Pallas kernels, per_device(): pl.pallas_call(middle_kernel, out_shape=[send_shape, normed_shape, turned...  7.65 us
    pallas_call x2, Pallas kernels, triangle(): pl.pallas_call(functools.partial(triangle_kernel, n_row, n_col, incoming)...  5.07 us

profile of v8, /device:TPU:0, one launch (start us, length us, event | category | flops | bytes accessed | tf_op | source)
XLA Modules:
  0.0 213.4 jit_solution(10993143165227496623)
XLA Ops:
  0.7 0.1 pad_add_fusion.place_ref
  0.7 0.0 copy-start.1
  0.7 0.0 copy-start.4
  0.7 0.0 copy-start.5
  0.7 3.4 %shard_map.73.standard_ref = f32[64,128,128]{2,1,0:T(8,128)S(1)} custom-call(s32[3]{0:T(128)S(1)} %pad_add_fusion.place_ref, f32[64,128,128]{2,1,0:T(8,128)} %state_ref.3), custom_call_target="tpu_custom_call" | custom-call | tf_op jit(solution)/shard_map/pallas_call | solution.py:394
  4.2 0.0 copy-done.1
  4.2 0.0 copy-done.4
  4.2 0.0 copy-done.5
  4.2 3.9 %shard_map.74 = (bf16[128,2,64,128]{3,2,1,0:T(8,128)(2,1)S(1)}, bf16[64,128,128]{2,1,0:T(8,128)(2,1)S(1)}) custom-call(s32[3]{0:T(128)S(1)} %pad_add_fusion.place_ref, f32[64,128,128]{2,1,0:T(8,128)S(1)} %shard_map.73.standard_ref, bf16[2,128,4,128]{3,2,1,0:T(4,128)(2,1)S(1)} %copy-done.1, f32[2,2,128]{2,1,0:T(2,128)S(1)} %copy-done.4, ...), custom_call_target="tpu_custom_call" | custom-call | tf_op jit(solution)/shard_map/pallas_call | solution.py:405
  8.1 63.0 %all_to_all.20.received_ref = bf16[128,2,64,128]{3,2,1,0:T(8,128)(2,1)S(1)} all-to-all(bf16[128,2,64,128]{3,2,1,0:T(8,128)(2,1)S(1)} %get-tuple-element.10), channel_id=1, replica_groups=mesh['row'=16,'col'=8] {'row','col'}, dimensions={0} | all-to-all | bytes 8388608 | tf_op jit(solution)/shard_map/all_to_all | solution.py:376
  71.1 0.0 copy-start
  71.1 0.0 copy-start.2
  71.1 0.0 copy-start.3
  71.1 2.5 %shard_map.75 = bf16[128,64,128]{2,1,0:T(8,128)(2,1)S(1)} custom-call(bf16[128,2,64,128]{3,2,1,0:T(8,128)(2,1)S(1)} %all_to_all.20.received_ref), custom_call_target="tpu_custom_call" | custom-call | tf_op jit(solution)/shard_map/pallas_call | solution.py:382
  73.6 34.3 %all_to_all.21.returned_ref = bf16[128,64,128]{2,1,0:T(8,128)(2,1)S(1)} all-to-all(bf16[128,64,128]{2,1,0:T(8,128)(2,1)S(1)} %shard_map.75), channel_id=1, replica_groups=mesh['row'=16,'col'=8] {'row','col'}, dimensions={0} | all-to-all | bytes 4194304 | tf_op jit(solution)/shard_map/all_to_all | solution.py:376
  108.0 0.0 copy-done
  108.0 0.0 copy-done.2
  108.0 0.0 copy-done.3
  108.0 7.7 %shard_map.76 = (bf16[128,2,64,128]{3,2,1,0:T(8,128)(2,1)S(1)}, bf16[64,128,128]{2,1,0:T(8,128)(2,1)S(1)}, f32[64,128,128]{2,1,0:T(8,128)S(1)}) custom-call(s32[3]{0:T(128)S(1)} %pad_add_fusion.place_ref, bf16[128,64,128]{2,1,0:T(8,128)(2,1)S(1)} %all_to_all.21.returned_ref, f32[64,128,128]{2,1,0:T(8,128)S(1)} %copy-done, ...), custom_call_target="tpu_custom_call" | custom-call | tf_op jit(solution)/shard_map/pallas_call | solution.py:415
  115.6 56.9 %all_to_all.22.received_ref = bf16[128,2,64,128]{3,2,1,0:T(8,128)(2,1)S(1)} all-to-all(bf16[128,2,64,128]{3,2,1,0:T(8,128)(2,1)S(1)} %get-tuple-element.12), channel_id=1, replica_groups=mesh['row'=16,'col'=8] {'row','col'}, dimensions={0} | all-to-all | bytes 8388608 | tf_op jit(solution)/shard_map/all_to_all | solution.py:376
  172.5 2.6 %shard_map.77 = bf16[128,64,128]{2,1,0:T(8,128)(2,1)S(1)} custom-call(bf16[128,2,64,128]{3,2,1,0:T(8,128)(2,1)S(1)} %all_to_all.22.received_ref), custom_call_target="tpu_custom_call" | custom-call | tf_op jit(solution)/shard_map/pallas_call | solution.py:382
  175.1 34.3 %all_to_all.23.returned_ref = bf16[128,64,128]{2,1,0:T(8,128)(2,1)S(1)} all-to-all(bf16[128,64,128]{2,1,0:T(8,128)(2,1)S(1)} %shard_map.77), channel_id=1, replica_groups=mesh['row'=16,'col'=8] {'row','col'}, dimensions={0} | all-to-all | bytes 4194304 | tf_op jit(solution)/shard_map/all_to_all | solution.py:376
  209.4 3.8 %shard_map.78 = f32[64,128,128]{2,1,0:T(8,128)} custom-call(bf16[128,64,128]{2,1,0:T(8,128)(2,1)S(1)} %all_to_all.23.returned_ref, f32[64,128,128]{2,1,0:T(8,128)S(1)} %get-tuple-element.13.state_ref, bf16[64,128,128]{2,1,0:T(8,128)(2,1)S(1)} %get-tuple-element.14.normed_in_ref, f32[2,2,128]{2,1,0:T(2,128)S(1)} %copy-done.4, f32[2,2,128]{2,1,0:T(2,128)S(1)} %copy-done.5, ...), custom_call_target="tpu_custom_call" | custom-call | tf_op jit(solution)/shard_map/pallas_call | solution.py:444
Async XLA Ops:
  0.7 3.4 %copy-start.1 = (bf16[2,128,4,128]{3,2,1,0:T(4,128)(2,1)S(1)}, bf16[2,128,4,128]{3,2,1,0:T(4,128)(2,1)}, u32[]{:S(2)}) copy-start(bf16[2,128,4,128]{3,2,1,0:T(4,128)(2,1)} %project_ref.3) | copy-start | bytes 786436
  0.7 3.5 %copy-start.4 = (f32[2,2,128]{2,1,0:T(2,128)S(1)}, f32[2,2,128]{2,1,0:T(2,128)}, u32[]{:S(2)}) copy-start(f32[2,2,128]{2,1,0:T(2,128)} %gain_ref.5) | copy-start | bytes 6148
  0.7 3.5 %copy-start.5 = (f32[2,2,128]{2,1,0:T(2,128)S(1)}, f32[2,2,128]{2,1,0:T(2,128)}, u32[]{:S(2)}) copy-start(f32[2,2,128]{2,1,0:T(2,128)} %bias_ref.5) | copy-start | bytes 6148
  71.1 36.8 %copy-start = (f32[64,128,128]{2,1,0:T(8,128)S(1)}, f32[64,128,128]{2,1,0:T(8,128)}, u32[]{:S(2)}) copy-start(f32[64,128,128]{2,1,0:T(8,128)} %state_ref.3) | copy-start | bytes 12582916
  71.1 36.8 %copy-start.2 = (bf16[2,128,128]{2,1,0:T(8,128)(2,1)S(1)}, bf16[2,128,128]{2,1,0:T(8,128)(2,1)}, u32[]{:S(2)}) copy-start(bf16[2,128,128]{2,1,0:T(8,128)(2,1)} %out_ref.3) | copy-start | bytes 196612
  71.1 36.8 %copy-start.3 = (bf16[2,128,128]{2,1,0:T(8,128)(2,1)S(1)}, bf16[2,128,128]{2,1,0:T(8,128)(2,1)}, u32[]{:S(2)}) copy-start(bf16[2,128,128]{2,1,0:T(8,128)(2,1)} %gate_ref.3) | copy-start | bytes 196612

commit v9 on v8

--- a/solution.py
+++ b/solution.py
@@ -109,7 +109,9 @@
     stat_scratch[block % 2, 1] = lax.rsqrt(jnp.maximum(variance, 0.0) + epsilon)
 
 
-def update_pair(row, normed_ref, affine_ref, out_ref, gate_ref, product_scratch, stat_scratch):
+def update_pair(
+    row, normed_ref, affine_ref, out_ref, gate_ref, product_scratch, stat_scratch, folded=False
+):
     channels = normed_ref.shape[1]
     block, at = block_pair(row)
     hidden = []
@@ -117,14 +119,25 @@
         values = product_scratch[block % 2, pl.ds(at + t, channels, stride=spaced), :]
         centre = stat_scratch[block % 2, 0, at + t : at + t + 1, :]
         scale = stat_scratch[block % 2, 1, at + t : at + t + 1, :]
-        out = (values - centre) * scale * affine_ref[0] + affine_ref[1]
+        out = (values - centre) * scale
+        if not folded:
+            out = out * affine_ref[0] + affine_ref[1]
         hidden.append(out.astype(jnp.bfloat16))
     term = jnp.dot(
         out_ref[...], jnp.concatenate(hidden, axis=1), preferred_element_type=jnp.float32
     )
     normed = jnp.concatenate([normed_ref[row], normed_ref[row + 1]], axis=1)
     gate = jnp.tanh(jnp.dot(gate_ref[...], normed, preferred_element_type=jnp.float32)) + 1.0
+    if folded:
+        term = term + jnp.concatenate([affine_ref[1], affine_ref[1]], axis=1)
     return gate * term
+
+
+def fold_affine(layer, place_in, affine_ref, place_out):
+    raw = place_in[layer].astype(jnp.float32) * 0.5
+    place_out[...] = (raw * affine_ref[0]).T.astype(jnp.bfloat16)
+    constant = jnp.sum(raw * affine_ref[1], axis=0, keepdims=True)
+    affine_ref[1] = jnp.broadcast_to(constant, raw.shape).T
 
 
 def fetch_kernel(place_ref, state_ref, standard_ref, state_buf, sems):
@@ -269,7 +282,7 @@
     n_blocks = n_rows // block_rows
     store_rows = n_rows // sems.shape[0]
     turn_affine(1, 1, gain_ref, bias_ref, affine_ref)
-    turn_weights(1, out_ref, out_weight_ref)
+    fold_affine(1, out_ref, affine_ref, out_weight_ref)
     turn_weights(1, gate_ref, gate_weight_ref)
     nothing = jnp.zeros((block_rows, cols), jnp.float32)
 
@@ -292,6 +305,7 @@
                     gate_weight_ref,
                     product_scratch,
                     stat_scratch,
+                    folded=True,
                 )
                 for t in range(2):
                     values = state_ref[row + t] + term[:, t * cols : (t + 1) * cols]

time: 214 us -> 213 us (level)
  no operation moved by 1% of the time
where the time goes in v9:
time: 213 us
  blocking collectives  189 us (89%)
  Pallas kernels  23.5 us (11%)
    all_to_all x4, blocking collectives, exchange(): return lax.all_to_all(blocks, mesh_axes, 0, 0, tiled=True)  189 us
    pallas_call x1, Pallas kernels, per_device(): pl.pallas_call(middle_kernel, out_shape=[send_shape, normed_shape, turned...  7.65 us
    pallas_call x2, Pallas kernels, triangle(): pl.pallas_call(functools.partial(triangle_kernel, n_row, n_col, incoming)...  5.07 us

profile of v9, /device:TPU:0, one launch (start us, length us, event | category | flops | bytes accessed | tf_op | source)
XLA Modules:
  0.0 213.1 jit_solution(16053704108021541861)
XLA Ops:
  0.7 0.1 pad_add_fusion.place_ref
  0.7 0.0 copy-start.1
  0.7 0.0 copy-start.4
  0.7 0.0 copy-start.5
  0.7 3.4 %shard_map.73.standard_ref = f32[64,128,128]{2,1,0:T(8,128)S(1)} custom-call(s32[3]{0:T(128)S(1)} %pad_add_fusion.place_ref, f32[64,128,128]{2,1,0:T(8,128)} %state_ref.3), custom_call_target="tpu_custom_call" | custom-call | tf_op jit(solution)/shard_map/pallas_call | solution.py:408
  4.2 0.0 copy-done.1
  4.2 0.0 copy-done.4
  4.2 0.0 copy-done.5
  4.2 3.9 %shard_map.74 = (bf16[128,2,64,128]{3,2,1,0:T(8,128)(2,1)S(1)}, bf16[64,128,128]{2,1,0:T(8,128)(2,1)S(1)}) custom-call(s32[3]{0:T(128)S(1)} %pad_add_fusion.place_ref, f32[64,128,128]{2,1,0:T(8,128)S(1)} %shard_map.73.standard_ref, bf16[2,128,4,128]{3,2,1,0:T(4,128)(2,1)S(1)} %copy-done.1, f32[2,2,128]{2,1,0:T(2,128)S(1)} %copy-done.4, ...), custom_call_target="tpu_custom_call" | custom-call | tf_op jit(solution)/shard_map/pallas_call | solution.py:419
  8.1 63.0 %all_to_all.20.received_ref = bf16[128,2,64,128]{3,2,1,0:T(8,128)(2,1)S(1)} all-to-all(bf16[128,2,64,128]{3,2,1,0:T(8,128)(2,1)S(1)} %get-tuple-element.10), channel_id=1, replica_groups=mesh['row'=16,'col'=8] {'row','col'}, dimensions={0} | all-to-all | bytes 8388608 | tf_op jit(solution)/shard_map/all_to_all | solution.py:390
  71.1 0.0 copy-start
  71.1 0.0 copy-start.2
  71.1 0.0 copy-start.3
  71.1 2.5 %shard_map.75 = bf16[128,64,128]{2,1,0:T(8,128)(2,1)S(1)} custom-call(bf16[128,2,64,128]{3,2,1,0:T(8,128)(2,1)S(1)} %all_to_all.20.received_ref), custom_call_target="tpu_custom_call" | custom-call | tf_op jit(solution)/shard_map/pallas_call | solution.py:396
  73.6 34.3 %all_to_all.21.returned_ref = bf16[128,64,128]{2,1,0:T(8,128)(2,1)S(1)} all-to-all(bf16[128,64,128]{2,1,0:T(8,128)(2,1)S(1)} %shard_map.75), channel_id=1, replica_groups=mesh['row'=16,'col'=8] {'row','col'}, dimensions={0} | all-to-all | bytes 4194304 | tf_op jit(solution)/shard_map/all_to_all | solution.py:390
  108.0 0.0 copy-done
  108.0 0.0 copy-done.2
  108.0 0.0 copy-done.3
  108.0 7.7 %shard_map.76 = (bf16[128,2,64,128]{3,2,1,0:T(8,128)(2,1)S(1)}, bf16[64,128,128]{2,1,0:T(8,128)(2,1)S(1)}, f32[64,128,128]{2,1,0:T(8,128)S(1)}) custom-call(s32[3]{0:T(128)S(1)} %pad_add_fusion.place_ref, bf16[128,64,128]{2,1,0:T(8,128)(2,1)S(1)} %all_to_all.21.returned_ref, f32[64,128,128]{2,1,0:T(8,128)S(1)} %copy-done, ...), custom_call_target="tpu_custom_call" | custom-call | tf_op jit(solution)/shard_map/pallas_call | solution.py:429
  115.6 56.9 %all_to_all.22.received_ref = bf16[128,2,64,128]{3,2,1,0:T(8,128)(2,1)S(1)} all-to-all(bf16[128,2,64,128]{3,2,1,0:T(8,128)(2,1)S(1)} %get-tuple-element.12), channel_id=1, replica_groups=mesh['row'=16,'col'=8] {'row','col'}, dimensions={0} | all-to-all | bytes 8388608 | tf_op jit(solution)/shard_map/all_to_all | solution.py:390
  172.5 2.6 %shard_map.77 = bf16[128,64,128]{2,1,0:T(8,128)(2,1)S(1)} custom-call(bf16[128,2,64,128]{3,2,1,0:T(8,128)(2,1)S(1)} %all_to_all.22.received_ref), custom_call_target="tpu_custom_call" | custom-call | tf_op jit(solution)/shard_map/pallas_call | solution.py:396
  175.1 34.3 %all_to_all.23.returned_ref = bf16[128,64,128]{2,1,0:T(8,128)(2,1)S(1)} all-to-all(bf16[128,64,128]{2,1,0:T(8,128)(2,1)S(1)} %shard_map.77), channel_id=1, replica_groups=mesh['row'=16,'col'=8] {'row','col'}, dimensions={0} | all-to-all | bytes 4194304 | tf_op jit(solution)/shard_map/all_to_all | solution.py:390
  209.4 3.5 %shard_map.78 = f32[64,128,128]{2,1,0:T(8,128)} custom-call(bf16[128,64,128]{2,1,0:T(8,128)(2,1)S(1)} %all_to_all.23.returned_ref, f32[64,128,128]{2,1,0:T(8,128)S(1)} %get-tuple-element.13.state_ref, bf16[64,128,128]{2,1,0:T(8,128)(2,1)S(1)} %get-tuple-element.14.normed_in_ref, f32[2,2,128]{2,1,0:T(2,128)S(1)} %copy-done.4, f32[2,2,128]{2,1,0:T(2,128)S(1)} %copy-done.5, ...), custom_call_target="tpu_custom_call" | custom-call | tf_op jit(solution)/shard_map/pallas_call | solution.py:458
Async XLA Ops:
  0.7 3.4 %copy-start.1 = (bf16[2,128,4,128]{3,2,1,0:T(4,128)(2,1)S(1)}, bf16[2,128,4,128]{3,2,1,0:T(4,128)(2,1)}, u32[]{:S(2)}) copy-start(bf16[2,128,4,128]{3,2,1,0:T(4,128)(2,1)} %project_ref.3) | copy-start | bytes 786436
  0.7 3.5 %copy-start.4 = (f32[2,2,128]{2,1,0:T(2,128)S(1)}, f32[2,2,128]{2,1,0:T(2,128)}, u32[]{:S(2)}) copy-start(f32[2,2,128]{2,1,0:T(2,128)} %gain_ref.5) | copy-start | bytes 6148
  0.7 3.5 %copy-start.5 = (f32[2,2,128]{2,1,0:T(2,128)S(1)}, f32[2,2,128]{2,1,0:T(2,128)}, u32[]{:S(2)}) copy-start(f32[2,2,128]{2,1,0:T(2,128)} %bias_ref.5) | copy-start | bytes 6148
  71.1 36.8 %copy-start = (f32[64,128,128]{2,1,0:T(8,128)S(1)}, f32[64,128,128]{2,1,0:T(8,128)}, u32[]{:S(2)}) copy-start(f32[64,128,128]{2,1,0:T(8,128)} %state_ref.3) | copy-start | bytes 12582916
  71.1 36.8 %copy-start.2 = (bf16[2,128,128]{2,1,0:T(8,128)(2,1)S(1)}, bf16[2,128,128]{2,1,0:T(8,128)(2,1)}, u32[]{:S(2)}) copy-start(bf16[2,128,128]{2,1,0:T(8,128)(2,1)} %out_ref.3) | copy-start | bytes 196612
  71.1 36.8 %copy-start.3 = (bf16[2,128,128]{2,1,0:T(8,128)(2,1)S(1)}, bf16[2,128,128]{2,1,0:T(8,128)(2,1)}, u32[]{:S(2)}) copy-start(bf16[2,128,128]{2,1,0:T(8,128)(2,1)} %gate_ref.3) | copy-start | bytes 196612
